TPU v7x, 256 devices: a whole 4x4x8 slice. The times are simulated.
256 devices in a mesh: dp: 4 (over z_hi), mp: 64 (over x, y, z_lo, core).
Axes of the slice: x: 4, y: 4, z: 8 (z_hi: 4, z_lo: 2; z = z_hi * 2 + z_lo), core: 2. Of those that a mesh axis runs over, the one named last changes fastest.
Arguments:
- activations: bfloat16 [1024, 4096], P('dp'), may hold values from -6 to 6
- cotangent: bfloat16 [1024, 8192], P('dp'), may hold values from -0.1875 to 0.1875
- owners: int32 [4, 64, 1], P('dp'), may hold values from 0 to 63; in each aligned block of 64 rows (0 to 63, 64 to 127, ..., all dimensions but the last counted through in order) at most 2 rows name the same one
- history: float32 [4, 64, 2, 512, 512], P('dp', 'mp'), as said below
Outputs:
- precond: float32 [128, 512, 512], P('mp', 'dp')
- new_history: float32 [4, 64, 2, 512, 512], P('dp', 'mp')
Inputs may be any that keep to these rules, and one draw needn't show every extreme that they name: `owners`: within the 64 rows of one dp index no owner is named more than 2 times, and in some dp index an owner is named exactly 2 times. `history`: every slot holds a symmetric positive definite matrix; slots beyond the statistics assigned to an owner are returned unchanged.
All inputs are finite; a program needn't handle non-finite values.
Results may differ from a plain program's by a relative error of at most 0.0003.
Values sent between devices are 32-bit elements; how exact they have to be, the bound alone decides.
A program may use at most 64 MiB of HBM per device.

v0:
```python
import jax
import jax.numpy as jnp
from jax import lax
from jax.sharding import PartitionSpec as P

D = 4096
FFW = 8192
B = 512
ITERS = 3


decay = 0.8
highest = lax.Precision.HIGHEST


def matmul(left, right):
    return jnp.matmul(left, right, precision=highest)


def inverse_root(matrices):
    order = matrices.shape[-1]
    ident = jnp.eye(order, dtype=matrices.dtype)
    norms = jnp.sqrt(jnp.sum(matrices * matrices, axis=(-2, -1), keepdims=True)) + 1e-06
    scale = 2.5 / norms
    iterate = ident * scale**0.25
    coupled = matrices * scale
    for iteration in range(ITERS):
        factor = (5.0 * ident - coupled) * 0.25
        iterate = matmul(iterate, factor)
        square = matmul(factor, factor)
        fourth = matmul(square, square)
        coupled = matmul(fourth, coupled)
    return iterate


def slot_ranks(owner_row):
    length = owner_row.shape[0]
    same = owner_row[:, None] == owner_row[None, :]
    earlier = jnp.arange(length)[None, :] < jnp.arange(length)[:, None]
    return jnp.sum(same & earlier, axis=1)


def send_back(payload, owner_row, ranks, count_mp, per_device, piece_rows):
    slot_total = payload.shape[0]
    split = payload.reshape(slot_total, count_mp, piece_rows, B)
    arrived = lax.all_to_all(split, "mp", split_axis=1, concat_axis=1, tiled=True)
    flat_arrived = arrived.reshape(slot_total * count_mp, piece_rows, B)
    member_grid = jnp.arange(count_mp)[None, :] * per_device + jnp.arange(per_device)[:, None]
    back_pick = jnp.take(ranks, member_grid) * count_mp + jnp.take(owner_row, member_grid)
    outgoing = jnp.take(flat_arrived, back_pick, axis=0)
    returned = lax.all_to_all(outgoing, "mp", split_axis=1, concat_axis=1, tiled=True)
    return returned.reshape(per_device, B, B)


def body(activations, cotangent, owners, history):
    count_dp = lax.axis_size("dp")
    count_mp = lax.axis_size("mp")
    dp_index = lax.axis_index("dp")
    mp_index = lax.axis_index("mp")
    band_count = D // B
    block_total = band_count * (FFW // B)
    blocks_here = block_total // count_mp
    per_device = 2 * blocks_here // count_dp
    slot_total = 2 * per_device
    piece_rows = B // count_mp
    block_ids = mp_index * blocks_here + jnp.arange(blocks_here, dtype=jnp.int32)
    row_bands = jnp.take(
        activations.reshape(activations.shape[0], band_count, B), block_ids % band_count, axis=1
    )
    col_bands = jnp.take(
        cotangent.reshape(cotangent.shape[0], FFW // B, B), block_ids // band_count, axis=1
    )
    partial_value = jnp.einsum(
        "tbi,tbj->bij", row_bands, col_bands, preferred_element_type=jnp.float32
    )
    gradient = lax.psum(partial_value, "dp")
    local_blocks = dp_index // 2 + count_dp // 2 * jnp.arange(per_device, dtype=jnp.int32)
    side_bit = dp_index % 2
    chosen = jnp.take(gradient, local_blocks, axis=0)
    oriented = jnp.where(side_bit == 0, chosen, jnp.swapaxes(chosen, 1, 2))
    fresh = matmul(oriented, jnp.swapaxes(oriented, 1, 2)) / B
    owner_row = owners[0, :, 0]
    ranks = slot_ranks(owner_row)
    group_size = owner_row.shape[0]
    members = jnp.arange(group_size, dtype=jnp.int32)
    piece_index = members % per_device * count_mp + members // per_device
    matched = (owner_row[None, None, :] == jnp.arange(count_mp)[:, None, None]) & (
        ranks[None, None, :] == jnp.arange(slot_total)[None, :, None]
    )
    pick = jnp.sum(jnp.where(matched, piece_index[None, None, :], 0), axis=2)
    used = jnp.any(matched, axis=2)
    pieces = fresh.reshape(per_device, count_mp, piece_rows, B)
    received = lax.all_to_all(pieces, "mp", split_axis=1, concat_axis=1, tiled=True)
    flat_pieces = received.reshape(per_device * count_mp, piece_rows, B)
    outgoing = jnp.take(flat_pieces, pick.T, axis=0)
    incoming = lax.all_to_all(outgoing, "mp", split_axis=1, concat_axis=1, tiled=True).reshape(
        slot_total, B, B
    )
    my_used = jnp.take(used, mp_index, axis=0)
    held = history[0, 0]
    merged = jnp.where(my_used[:, None, None], decay * held + (1.0 - decay) * incoming, held)
    new_history = merged.reshape(1, 1, slot_total, B, B)
    payload = inverse_root(merged)
    returned = send_back(payload, owner_row, ranks, count_mp, per_device, piece_rows)
    every = lax.all_gather(returned.reshape(per_device, 1, B, B), "dp", axis=1, tiled=True)
    paired = every.reshape(blocks_here, 2, B, B)
    row_count = B // count_dp
    left_rows = lax.dynamic_slice_in_dim(paired[:, 0], dp_index * row_count, row_count, 1)
    result = matmul(matmul(left_rows, gradient), paired[:, 1])
    return (result, new_history)


def solution(mesh):
    return jax.shard_map(
        body,
        mesh=mesh,
        in_specs=(
            P("dp", None),
            P("dp", None),
            P("dp", None, None),
            P("dp", "mp", None, None, None),
        ),
        out_specs=(P("mp", "dp", None), P("dp", "mp", None, None, None)),
        check_vma=False,
    )
```

profile of v0, /device:TPU:37, one launch (start us, length us, event | category | flops | bytes accessed | tf_op | source)
XLA Modules:
  0.0 401.5 jit_solution(6874856912245030246)
XLA Ops:
  7.2 0.0 all-reduce.2.cloned.1.call-start
  7.3 6.4 %copy.49 = bf16[256,8192]{0,1:T(8,128)(2,1)} copy(bf16[256,8192]{1,0:T(8,128)(2,1)} %param.7) | data formatting | bytes 8388608 | tf_op args[1]
  13.7 6.4 %copy.50 = bf16[256,16,512]{2,0,1:T(8,128)(2,1)} copy(bf16[256,16,512]{0,2,1:T(8,128)(2,1)} %bitcast.111) | data formatting | bytes 8388608 | tf_op jit(solution)/shard_map/reshape | solution.py:71
  20.1 3.3 copy.47
  23.4 2.4 copy.48
  25.8 2.8 gather_fusion.1
  28.6 2.2 gather_fusion
  30.7 1.9 fusion.39
  32.6 0.0 all-reduce.2.cloned.1.call-update
  32.7 102.5 %all-reduce.2.cloned.1.call-done = f32[2,512,512]{2,1,0:T(8,128)} async-done(((f32[2,512,512]{2,1,0:T(8,128)}), f32[2,512,512]{2,1,0:T(8,128)}) %all-reduce.2.cloned.1.call-update) | async-done | bytes 2097168 | tf_op jit(solution)/shard_map/psum | solution.py:76
  135.2 1.3 dynamic-slice_select_fusion
  136.5 0.3 copy.52
  136.9 2.9 fusion.16
  139.8 0.0 copy-start
  139.8 9.1 %all-to-all-start = ((f32[1,64,8,512]{3,2,0,1:T(8,128)}), f32[1,64,8,512]{3,2,0,1:T(8,128)S(1)}, u32[]{:S(2)}, u32[]{:S(2)}) async-start(f32[1,64,8,512]{3,2,0,1:T(8,128)} %fusion.16), calls=%async_computation | async-start | bytes 2097152 | tf_op jit(solution)/shard_map/all_to_all | solution.py:93
  148.9 0.0 copy-done
  148.9 0.2 convert_reduce_fusion
  149.1 0.1 fusion.49
  149.2 0.1 reshape.370
  149.3 0.1 copy.46
  149.4 14.5 %all-to-all-done = f32[1,64,8,512]{3,2,0,1:T(8,128)S(1)} async-done(((f32[1,64,8,512]{3,2,0,1:T(8,128)}), f32[1,64,8,512]{3,2,0,1:T(8,128)S(1)}, u32[]{:S(2)}, u32[]{:S(2)}) %all-to-all-start) | async-done | bytes 1048608 | tf_op jit(solution)/shard_map/all_to_all | solution.py:93
  163.9 2.1 gather_fusion.2
  166.1 3.1 copy_select_fusion
  169.2 8.6 %all-to-all-start.1 = ((f32[2,64,8,512]{3,2,0,1:T(8,128)}), f32[2,64,8,512]{3,2,0,1:T(8,128)S(1)}, u32[]{:S(2)}, u32[]{:S(2)}) async-start(f32[2,64,8,512]{3,2,0,1:T(8,128)} %copy_select_fusion), calls=%async_computation.1 | async-start | bytes 4194304 | tf_op jit(solution)/shard_map/all_to_all | solution.py:96
  177.8 0.1 and_reduce_fusion
  177.9 0.2 select_reduce_fusion
  178.1 0.1 fusion.35
  178.2 1.1 fusion.36
  179.3 24.7 %all-to-all-done.1 = f32[2,64,8,512]{3,2,0,1:T(8,128)S(1)} async-done(((f32[2,64,8,512]{3,2,0,1:T(8,128)}), f32[2,64,8,512]{3,2,0,1:T(8,128)S(1)}, u32[]{:S(2)}, u32[]{:S(2)}) %all-to-all-start.1) | async-done | bytes 2097184 | tf_op jit(solution)/shard_map/all_to_all | solution.py:96
  204.0 2.2 multiply_reduce_fusion
  206.2 4.0 %fusion.12 = f32[2,512,512]{2,1,0:T(8,128)S(1)} fusion(f32[2,512,512]{2,1,0:T(8,128)S(1)} %get-tuple-element.28, f32[2]{0:T(128)S(1)} %get-tuple-element.26, f32[512,512]{1,0:T(8,128)S(1)} %fusion.35), kind=kOutput, calls=%fused_computation.27 | convolution fusion | flops 3222798336 | bytes 5242888 | tf_op jit(solution)/shard_map/dot_general | solution.py:17
  210.3 3.5 fusion.64
  213.8 3.7 fusion.8
  217.5 0.0 copy-start.3
  217.5 4.0 fusion.10
  221.5 0.0 copy-done.3
  221.5 3.9 fusion.6
  225.4 3.7 fusion.11
  229.1 3.5 fusion.65
  232.7 3.8 fusion.66
  236.4 3.7 fusion.13
  240.2 1.5 copy.56
  241.7 8.2 %all-to-all-start.2 = ((f32[2,64,8,512]{3,2,0,1:T(8,128)}), f32[2,64,8,512]{3,2,0,1:T(8,128)}, u32[]{:S(2)}, u32[]{:S(2)}) async-start(f32[2,64,8,512]{3,2,0,1:T(8,128)} %copy.56), calls=%async_computation.2 | async-start | bytes 4194304 | tf_op jit(solution)/shard_map/all_to_all | solution.py:46
  249.9 0.0 all-gather.2.cloned.1.call-start
  250.0 0.8 gather_fusion.5
  250.7 0.8 gather_fusion.4
  251.6 25.0 %all-to-all-done.2 = f32[2,64,8,512]{3,2,0,1:T(8,128)} async-done(((f32[2,64,8,512]{3,2,0,1:T(8,128)}), f32[2,64,8,512]{3,2,0,1:T(8,128)}, u32[]{:S(2)}, u32[]{:S(2)}) %all-to-all-start.2) | async-done | bytes 2097184 | tf_op jit(solution)/shard_map/all_to_all | solution.py:46
  276.5 3.1 copy.57
  279.6 2.2 gather_fusion.3
  281.9 0.1 fusion.18
  282.0 23.2 %all_to_all.20 = f32[1,64,8,512]{3,2,0,1:T(8,128)} all-to-all(f32[1,64,8,512]{3,2,0,1:T(8,128)S(1)} %fusion.18), channel_id=1, replica_groups=mesh['dp'=4,'mp'=64] {'mp'}, dimensions={1} | all-to-all | bytes 2097152 | tf_op jit(solution)/shard_map/all_to_all | solution.py:51
  305.2 0.0 all-gather.2.cloned.1.call-update
  305.2 3.5 fusion.1
  308.7 80.0 %all-gather.2.cloned.1.call-done = f32[1,4,512,512]{3,2,0,1:T(8,128)} async-done(((f32[1,1,512,512]{3,2,0,1:T(8,128)}), f32[1,4,512,512]{3,2,0,1:T(8,128)}) %all-gather.2.cloned.1.call-update) | async-done | bytes 4194320 | tf_op jit(solution)/shard_map/all_gather | solution.py:105
  388.8 0.0 copy-start.1
  388.8 0.0 copy-start.2
  388.8 1.9 slice.36
  390.7 0.3 copy-done.1
  391.0 1.3 fusion.37
  392.3 0.0 copy-done.2
  392.3 2.1 fusion
  (15 shorter events, 0.1 us)
Async XLA Ops:
  7.2 128.1 %all-reduce.2.cloned.1.call-start = ((), (), s32[]{:S(2)}) async-start(), calls=%async_computation.4 | async-start | bytes 4194304 | tf_op jit(solution)/shard_map/psum | solution.py:76
  139.8 9.1 %copy-start = (s32[1,64,1]{1,2,0:T(1,128)S(1)}, s32[1,64,1]{1,2,0:T(1,128)}, u32[]{:S(2)}) copy-start(s32[1,64,1]{1,2,0:T(1,128)} %param.8) | copy-start | bytes 772
  139.8 24.2 %all-to-all-start = ((f32[1,64,8,512]{3,2,0,1:T(8,128)}), f32[1,64,8,512]{3,2,0,1:T(8,128)S(1)}, u32[]{:S(2)}, u32[]{:S(2)}) async-start(f32[1,64,8,512]{3,2,0,1:T(8,128)} %fusion.16), calls=%async_computation | async-start | bytes 2097152 | tf_op jit(solution)/shard_map/all_to_all | solution.py:93
  169.2 34.8 %all-to-all-start.1 = ((f32[2,64,8,512]{3,2,0,1:T(8,128)}), f32[2,64,8,512]{3,2,0,1:T(8,128)S(1)}, u32[]{:S(2)}, u32[]{:S(2)}) async-start(f32[2,64,8,512]{3,2,0,1:T(8,128)} %copy_select_fusion), calls=%async_computation.1 | async-start | bytes 4194304 | tf_op jit(solution)/shard_map/all_to_all | solution.py:96
  217.5 4.0 copy-start.3
  241.7 34.8 %all-to-all-start.2 = ((f32[2,64,8,512]{3,2,0,1:T(8,128)}), f32[2,64,8,512]{3,2,0,1:T(8,128)}, u32[]{:S(2)}, u32[]{:S(2)}) async-start(f32[2,64,8,512]{3,2,0,1:T(8,128)} %copy.56), calls=%async_computation.2 | async-start | bytes 4194304 | tf_op jit(solution)/shard_map/all_to_all | solution.py:46
  249.9 138.9 %all-gather.2.cloned.1.call-start = ((), (), s32[]{:S(2)}) async-start(), calls=%async_computation.5 | async-start | bytes 5242880 | tf_op jit(solution)/shard_map/all_gather | solution.py:105
  388.8 2.2 copy-start.1
  388.8 3.5 copy-start.2
Sparse Core Ops, SparseCore 0:
  32.8 102.3 all-reduce.1
  305.3 83.4 all-gather.1
where the time goes:
time: 408 us; the launch traced here: 402 us
  waiting for transfers between devices  247 us (61%)
  matrix products  42 us (10%)
  local copies, waits for them, and re-layouts  36.7 us (9%)
  starting transfers between devices  25.9 us (6%)
  blocking collectives  23.2 us (6%)
  between operations  14.6 us (4%)
  other arithmetic  12.3 us (3%)
    psum x1, waiting for transfers between devices, body(): gradient = lax.psum(partial_value, 'dp')  103 us
    all_gather x1, waiting for transfers between devices, body(): lax.all_gather(returned.reshape(per_device, 1, B, B), 'dp', axis=1, tiled...  80 us
    dot_general x12, matrix products, matmul(): return jnp.matmul(left, right, precision=highest)  40.1 us
    all_to_all x1, waiting for transfers between devices, send_back(): lax.all_to_all(split, 'mp', split_axis=1, concat_axis=1, tiled=True)  25 us
    all_to_all x1, waiting for transfers between devices, body(): lax.all_to_all(outgoing, 'mp', split_axis=1, concat_axis=1, tiled=True)  24.7 us
    all_to_all x1, blocking collectives, send_back(): lax.all_to_all(outgoing, 'mp', split_axis=1, concat_axis=1, tiled=True)  23.2 us
    all_to_all x1, waiting for transfers between devices, body(): lax.all_to_all(pieces, 'mp', split_axis=1, concat_axis=1, tiled=True)  14.5 us
    unnamed x10, local copies, waits for them, and re-layouts  9.99 us
  transfers between devices with their start and end apart: 5, of which 5 were waited for; matrix products, arithmetic and copies ran while one was open for 2% of the time, Pallas kernels for 0%

commit v1 on v0

v1 whole, which is shorter than its diff:
```python
import jax
import jax.numpy as jnp
from jax import lax
from jax.experimental import pallas as pl
from jax.experimental.pallas import tpu as pltpu
from jax.sharding import PartitionSpec as P

B = 512
Q = 128
UPPER = [(i, j) for i in range(4) for j in range(i, 4)]
ROWS = len(UPPER) * Q
CHIP_ROWS = 40
PIECE = (24, 16)
START = (0, 24)
f32 = jnp.float32
bf16 = jnp.bfloat16


def split(x):
    hi = x.astype(bf16)
    return hi, (x - hi.astype(f32)).astype(bf16)


def dot(a, b, dims=((1,), (0,))):
    return lax.dot_general(a, b, (dims, ((), ())), preferred_element_type=f32)


def dot3(ah, al, bh, bl, dims=((1,), (0,))):
    return dot(ah, bh, dims) + (dot(ah, bl, dims) + dot(al, bh, dims))


def kernel(
    act, cot, hist, table, prec, newh,
    act_own, act_part, cot_own, zact, zcot, act_full, cot_full,
    hv, hpk, hrecv, hsend, hfin, fpk, frecv, fsend, ffin,
    gtmp, gp, fbuf, xs, mats, pbuf, pfin,
    lsem, zsem, asem, csem, h1sem, h2sem, f1sem, f2sem, gsem, xsem, psend, precv,
):
    k = lax.axis_index("dp")
    mp = lax.axis_index("mp")
    s = lax.rem(mp, 2)
    chip = lax.div(mp, 2)
    zl = lax.rem(chip, 2)
    c = lax.div(mp, 4)
    w = lax.rem(mp, 4)
    par = lax.rem(k, 2)
    j = lax.div(k, 2)
    k1 = k + 1 - 2 * par
    mp1 = mp + 1 - 2 * s
    mp2 = mp + 2 - 4 * zl
    main = s == par

    def remote(src, dst, send, recv, dp_to, mp_to):
        return pltpu.make_async_remote_copy(
            src_ref=src, dst_ref=dst, send_sem=send, recv_sem=recv,
            device_id=(dp_to, mp_to), device_id_type=pl.DeviceIdType.MESH,
        )

    def wait_bytes(view, sem):
        pltpu.make_async_copy(view, view, sem).wait()

    def by_core(fn):
        for core in (0, 1):
            pl.when(s == core)(lambda core=core: fn(core, PIECE[core]))

    def spread(src_of, dst_of, send, recv):
        def to_chip(step, _):
            chip_to = lax.rem(chip + step, 32)
            for core in (0, 1):
                src = src_of(chip_to, core)
                remote(src, dst_of(core), send, recv, k, 2 * chip_to + core).start()
            return 0

        lax.fori_loop(1, 32, to_chip, 0)
        for core in (0, 1):

            @pl.when(s == core)
            def _(core=core):
                pltpu.make_async_copy(src_of(chip, core), dst_of(core), recv).start()
                other = 1 - core
                remote(src_of(chip, other), dst_of(other), send, recv, k, mp1).start()

    lefts = [
        pltpu.make_async_copy(hist, hv, lsem.at[0]),
        pltpu.make_async_copy(act.at[:, pl.ds((4 * zl + 2 * s + j) * B, B)], act_own, lsem.at[1]),
        pltpu.make_async_copy(cot.at[:, pl.ds(c * B, B)], cot_own, lsem.at[2]),
    ]
    for jj in (0, 1):
        band = (4 * zl + 2 * s + jj) * B
        lefts.append(
            pltpu.make_async_copy(
                act.at[pl.ds(c * 16, 16), pl.ds(band, B)], act_part.at[jj], lsem.at[3 + jj]
            )
        )
    for copy in lefts[::-1]:
        copy.start()
    for copy in lefts[1:][::-1]:
        copy.wait()
    zact[...] = act_part[...].astype(f32)
    zcot[...] = cot_own[pl.ds(pl.multiple_of(w * 64, 64), 64), :].astype(f32)
    mine_act = pl.ds(pl.multiple_of(c * 16, 16), 16)
    mine_cot = pl.ds(pl.multiple_of(w * 64, 64), 64)
    zcopies = []
    for e in (1, 2, 3):
        to = lax.rem(k + e, 4)
        zcopies.append(
            remote(
                zact.at[lax.div(to, 2)], act_full.at[3 - e, mine_act, :],
                zsem.at[0], zsem.at[1], to, mp,
            )
        )
        zcopies.append(
            remote(zcot, cot_full.at[3 - e, mine_cot, :], zsem.at[2], zsem.at[3], to, mp)
        )
    for copy in zcopies:
        copy.start()
    lefts[0].wait()
    for r in (0, 1):
        for n, (bi, bj) in enumerate(UPPER):
            hpk[r, pl.ds(n * Q, Q), :] = hv[r, pl.ds(bi * Q, Q), pl.ds(bj * Q, Q)]

    def piece_rows(chip_to, core):
        return pl.ds(pl.multiple_of(chip_to * CHIP_ROWS + START[core], 8), PIECE[core])

    spread(
        lambda chip_to, core: hpk.at[:, piece_rows(chip_to, core), :],
        lambda core: hrecv.at[pl.ds(2 * mp, 2), pl.ds(0, PIECE[core]), :],
        h1sem.at[0],
        h1sem.at[1],
    )
    wait_bytes(act_full.at[:, mine_act, :], zsem.at[1])
    part = act_full.at[:, mine_act, :]

    def to_plane(step, _):
        remote(part, part, asem.at[0], asem.at[1], k, lax.rem(mp + 4 * step, 64)).start()
        return 0

    lax.fori_loop(1, 16, to_plane, 0)
    wait_bytes(cot_full.at[:, mine_cot, :], zsem.at[3])
    part_cot = cot_full.at[:, mine_cot, :]
    across = remote(part_cot, part_cot, csem.at[0], csem.at[1], k, mp2)
    beside = remote(part_cot, part_cot, csem.at[2], csem.at[3], k, mp1)
    across.start()
    beside.start()
    far_cot = cot_full.at[:, pl.ds(pl.multiple_of(lax.rem(w + 2, 4) * 64, 64), 64), :]
    onward = remote(far_cot, far_cot, csem.at[4], csem.at[5], k, mp1)
    across.wait_recv()
    onward.start()

    def second_hop(core, rows):
        wait_bytes(hrecv.at[:, pl.ds(0, rows), :], h1sem.at[1])

        def choose(g, _):
            hsend[g, pl.ds(0, rows), :] = hrecv[table[g], pl.ds(0, rows), :]
            return 0

        lax.fori_loop(0, 64, choose, 0)
        dst = hfin.at[piece_rows(chip, core), :]

        def to_chip(step, _):
            chip_to = lax.rem(chip + step, 32)
            src = hsend.at[2 * chip_to + par, pl.ds(0, rows), :]
            remote(src, dst, h2sem.at[0], h2sem.at[1], k, 2 * chip_to + par).start()
            return 0

        lax.fori_loop(1, 32, to_chip, 0)

        def to_chip_beyond(step, _):
            chip_to = lax.rem(chip + step, 32)
            src = hsend.at[2 * chip_to + 1 - par, pl.ds(0, rows), :]
            remote(src, dst, h2sem.at[0], h2sem.at[1], k1, 2 * chip_to + par).start()
            return 0

        lax.fori_loop(0, 32, to_chip_beyond, 0)
        src = hsend.at[2 * chip + par, pl.ds(0, rows), :]

        @pl.when(main)
        def _():
            pltpu.make_async_copy(src, dst, h2sem.at[1]).start()

        @pl.when(jnp.logical_not(main))
        def _():
            remote(src, dst, h2sem.at[0], h2sem.at[1], k, mp1).start()

    by_core(second_hop)

    beside.wait_recv()
    onward.wait_recv()
    wait_bytes(act_full.at[:, pl.ds(0, 240), :], asem.at[1])
    down = ((0,), (0,))
    for half in (0, 1):
        rows = pl.ds(half * 256, 256)
        total = dot(act_own[:, rows], cot_own[...], down)
        for e in range(3):
            total += dot(
                act_full[e, :, rows].astype(bf16), cot_full[e].astype(bf16), down
            )
        gtmp[rows, :] = total
    send_g = remote(gtmp, gp, gsem.at[0], gsem.at[1], k, mp1)

    @pl.when(main)
    def _():
        send_g.start()
        gp[...] = gtmp[...]

    gh, gl = mats.at[0], mats.at[1]

    def fresh(g_ref, side):
        hi, lo = split(g_ref[...])
        gh[...] = hi
        gl[...] = lo
        for which, dims in ((0, ((1,), (1,))), (1, ((0,), (0,)))):

            @pl.when(side == which)
            def _(dims=dims):
                fbuf[...] = dot3(gh[...], gl[...], gh[...], gl[...], dims) * (1.0 / B)

    fresh(gtmp, par)
    for n, (bi, bj) in enumerate(UPPER):
        fpk[pl.ds(n * Q, Q), :] = fbuf[pl.ds(bi * Q, Q), pl.ds(bj * Q, Q)]
    spread(
        lambda chip_to, core: fpk.at[piece_rows(chip_to, core), :],
        lambda core: frecv.at[mp, pl.ds(0, PIECE[core]), :],
        f1sem.at[0],
        f1sem.at[1],
    )

    @pl.when(jnp.logical_not(main))
    def _():
        send_g.wait_recv()
        fresh(gp, s)

    wait_bytes(hfin, h2sem.at[1])
    for n, (bi, bj) in enumerate(UPPER):
        up = (pl.ds(bi * Q, Q), pl.ds(bj * Q, Q))
        block = 0.8 * hfin[pl.ds(n * Q, Q), :] + 0.2 * fbuf[up]
        fbuf[up] = block
        if bi != bj:
            fbuf[up[1], up[0]] = block.T
    square = jnp.sum(fbuf[...] * fbuf[...], axis=0, keepdims=True)
    norm = jnp.sqrt(jnp.sum(square, axis=1, keepdims=True)) + 1e-06
    scale = 2.5 / norm
    root_scale = jnp.sqrt(jnp.sqrt(scale))

    def store(slot, rows, value):
        hi, lo = split(value)
        mats[slot, rows, :] = hi
        mats[slot + 1, rows, :] = lo

    def factor(rows, start, value):
        row = start + lax.broadcasted_iota(jnp.int32, value.shape, 0)
        col = lax.broadcasted_iota(jnp.int32, value.shape, 1)
        return jnp.where(row == col, 1.25, 0.0) - 0.25 * value

    def product(a, b, after):
        for start in (0, 256):
            rows = pl.ds(start, 256)
            after(
                rows,
                start,
                dot3(mats[a, rows, :], mats[a + 1, rows, :], mats[b], mats[b + 1]),
            )

    MG, MQ, MS, MF, MM, MX, MR = 0, 2, 4, 6, 8, 10, 12
    for start in (0, 256):
        rows = pl.ds(start, 256)
        value = fbuf[rows, :] * scale
        store(MM, rows, value)
        store(MX, rows, factor(rows, start, value))
    product(MX, MX, lambda rows, start, value: store(MS, rows, value))
    product(MS, MS, lambda rows, start, value: store(MF, rows, value))

    def owners_hop(core, rows):
        wait_bytes(frecv.at[:, pl.ds(0, rows), :], f1sem.at[1])

        def choose(slot, _):
            o = lax.div(slot, 2)
            r = lax.rem(slot, 2)
            fsend[o, r, pl.ds(0, rows), :] = frecv[table[64 + slot], pl.ds(0, rows), :]
            return 0

        lax.fori_loop(0, 128, choose, 0)
        dst = ffin.at[:, piece_rows(chip, core), :]

        def to_owner(step, _):
            o = lax.rem(mp + step, 64)
            remote(
                fsend.at[o, :, pl.ds(0, rows), :], dst, f2sem.at[0], f2sem.at[1], k, o
            ).start()
            return 0

        lax.fori_loop(1, 64, to_owner, 0)
        pltpu.make_async_copy(fsend.at[mp, :, pl.ds(0, rows), :], dst, f2sem.at[1]).start()

    by_core(owners_hop)

    def next_step(rows, start, value):
        store(MR, rows, value)
        store(MQ, rows, factor(rows, start, value))

    product(MF, MM, next_step)
    product(MX, MQ, lambda rows, start, value: store(MM, rows, value))
    product(MQ, MQ, lambda rows, start, value: store(MS, rows, value))
    product(MS, MS, lambda rows, start, value: store(MF, rows, value))
    product(
        MF, MR, lambda rows, start, value: store(MQ, rows, factor(rows, start, value))
    )

    def last(rows, start, value):
        xs[s, rows, :] = value * root_scale

    product(MM, MQ, last)
    send_x = remote(xs.at[s], xs.at[s], xsem.at[0], xsem.at[1], k, mp1)
    send_x.start()
    store(MG, pl.ds(0, B), gp[...])
    send_x.wait_recv()

    store(MX, pl.ds(0, B), xs[1])
    copies = []
    for e in (0, 1):
        to = s + 2 * e
        hi, lo = split(xs[0, pl.ds(pl.multiple_of(to * Q, Q), Q), :])
        hi, lo = split(dot3(hi, lo, mats[MG], mats[MG + 1]))
        pbuf[e] = dot3(hi, lo, mats[MX], mats[MX + 1])
        copy = remote(pbuf.at[e], pfin.at[j], psend.at[e], precv.at[j], to, 2 * chip + par)
        away = jnp.logical_not(jnp.logical_and(main, to == k))
        pl.when(away)(copy.start)

        @pl.when(jnp.logical_not(away))
        def _(e=e):
            pfin[j] = pbuf[e]

        copies.append((copy, away))

    wait_bytes(ffin, f2sem.at[1])
    for r in (0, 1):
        used = table[192 + 2 * mp + r] > 0
        for n, (bi, bj) in enumerate(UPPER):
            up = (r, pl.ds(bi * Q, Q), pl.ds(bj * Q, Q))
            block = 0.2 * ffin[r, pl.ds(n * Q, Q), :]
            held = hv[up]
            hv[up] = jnp.where(used, 0.8 * held + block, held)
            if bi != bj:
                low = (r, up[2], up[1])
                held = hv[low]
                hv[low] = jnp.where(used, 0.8 * held + block.T, held)
    out_h = pltpu.make_async_copy(hv, newh, lsem.at[0])
    out_h.start()
    for jj in (0, 1):

        @pl.when(2 * jj + s != k)
        def _(jj=jj):
            wait_bytes(pfin.at[jj], precv.at[jj])

    out_p = pltpu.make_async_copy(pfin, prec, lsem.at[1])
    out_p.start()

    wait_bytes(act_full.at[:, pl.ds(0, 16), :], zsem.at[0])
    wait_bytes(cot_full.at[:, pl.ds(0, 64), :], zsem.at[2])
    wait_bytes(act_full.at[:, pl.ds(0, 240), :], asem.at[0])
    across.wait_send()
    beside.wait_send()
    onward.wait_send()

    def sent(core, rows):
        wait_bytes(hpk.at[:, pl.ds(0, ROWS - rows), :], h1sem.at[0])
        wait_bytes(fpk.at[pl.ds(0, ROWS - rows), :], f1sem.at[0])
        wait_bytes(fsend.at[pl.ds(0, 63), :, pl.ds(0, rows), :], f2sem.at[0])

        @pl.when(main)
        def _():
            wait_bytes(hsend.at[pl.ds(0, 63), pl.ds(0, rows), :], h2sem.at[0])

        @pl.when(jnp.logical_not(main))
        def _():
            wait_bytes(hsend.at[:, pl.ds(0, rows), :], h2sem.at[0])

    by_core(sent)
    pl.when(main)(send_g.wait_send)
    send_x.wait_send()
    for copy, away in copies:
        pl.when(away)(copy.wait_send)
    out_h.wait()
    out_p.wait()


def body(activations, cotangent, owners, history):
    owner_row = owners[0, :, 0]
    count = owner_row.shape[0]
    ids = jnp.arange(count, dtype=jnp.int32)
    same = owner_row[:, None] == owner_row[None, :]
    ranks = jnp.sum(same & (ids[None, :] < ids[:, None]), axis=1, dtype=jnp.int32)
    pick = owner_row * 2 + ranks
    slots = jnp.arange(2 * count, dtype=jnp.int32)
    matched = pick[None, :] == slots[:, None]
    source = jnp.sum(jnp.where(matched, ids[None, :], 0), axis=1, dtype=jnp.int32)
    used = jnp.sum(matched, axis=1, dtype=jnp.int32)
    table = jnp.concatenate([pick, source, used])
    anywhere = pl.BlockSpec(memory_space=pl.ANY)
    dma = pltpu.SemaphoreType.DMA
    prec, newh = pl.pallas_call(
        kernel,
        out_shape=[
            jax.ShapeDtypeStruct((2, 128, B), f32),
            jax.ShapeDtypeStruct((2, B, B), f32),
        ],
        in_specs=[anywhere, anywhere, anywhere, pl.BlockSpec(memory_space=pltpu.SMEM)],
        out_specs=[anywhere, anywhere],
        scratch_shapes=[
            pltpu.VMEM((256, B), bf16),
            pltpu.VMEM((2, 16, B), bf16),
            pltpu.VMEM((256, B), bf16),
            pltpu.VMEM((2, 16, B), f32),
            pltpu.VMEM((64, B), f32),
            pltpu.VMEM((3, 256, B), f32),
            pltpu.VMEM((3, 256, B), f32),
            pltpu.VMEM((2, B, B), f32),
            pltpu.VMEM((2, ROWS, Q), f32),
            pltpu.VMEM((128, 24, Q), f32),
            pltpu.VMEM((64, 24, Q), f32),
            pltpu.VMEM((ROWS, Q), f32),
            pltpu.VMEM((ROWS, Q), f32),
            pltpu.VMEM((64, 24, Q), f32),
            pltpu.VMEM((64, 2, 24, Q), f32),
            pltpu.VMEM((2, ROWS, Q), f32),
            pltpu.VMEM((B, B), f32),
            pltpu.VMEM((B, B), f32),
            pltpu.VMEM((B, B), f32),
            pltpu.VMEM((2, B, B), f32),
            pltpu.VMEM((14, B, B), bf16),
            pltpu.VMEM((2, 128, B), f32),
            pltpu.VMEM((2, 128, B), f32),
            dma((5,)),
            dma((4,)),
            dma((2,)),
            dma((6,)),
            dma((2,)),
            dma((2,)),
            dma((2,)),
            dma((2,)),
            dma((2,)),
            dma((2,)),
            dma((2,)),
            dma((2,)),
        ],
        compiler_params=pltpu.CompilerParams(
            has_side_effects=True, vmem_limit_bytes=48 * 1024 * 1024
        ),
    )(activations, cotangent, history[0, 0], table)
    return prec, newh[None, None]


def solution(mesh):
    return jax.shard_map(
        body,
        mesh=mesh,
        in_specs=(
            P("dp", None),
            P("dp", None),
            P("dp", None, None),
            P("dp", "mp", None, None, None),
        ),
        out_specs=(P("mp", "dp", None), P("dp", "mp", None, None, None)),
        check_vma=False,
    )
```

time: 408 us -> 125 us (0.31)
  the two profiles are of different devices: /device:TPU:37 before, /device:TPU:5 now
where the time goes in v1:
time: 125 us
  Pallas kernels  119 us (95%)
  local copies, waits for them, and re-layouts  3.71 us (3%)
  other arithmetic  1.75 us (1%)
    pallas_call x1, Pallas kernels, body(): pl.pallas_call(kernel, out_shape=[jax.ShapeDtypeStruct((2, 128, B), f32),...  119 us
    unnamed x4, local copies, waits for them, and re-layouts  3.71 us

profile of v1, /device:TPU:5, one launch (start us, length us, event | category | flops | bytes accessed | tf_op | source)
XLA Modules:
  0.0 125.0 jit_solution(17457694125572761649)
XLA Ops:
  0.6 0.9 convert_reduce_fusion.1
  1.5 0.7 multiply_add_fusion
  2.2 0.1 select_reduce_fusion
  2.3 0.1 pad_add_fusion.table
  2.4 0.0 copy-start
  2.4 1.6 %copy-done = bf16[256,4096]{1,0:T(8,128)(2,1)S(1)} copy-done((bf16[256,4096]{1,0:T(8,128)(2,1)S(1)}, bf16[256,4096]{1,0:T(8,128)(2,1)}, u32[]{:S(2)}) %copy-start) | copy-done | bytes 2097176
  4.0 118.9 %shard_map.59 = (f32[2,128,512]{2,1,0:T(8,128)S(1)}, f32[2,512,512]{2,1,0:T(8,128)S(1)}) custom-call(bf16[256,4096]{1,0:T(8,128)(2,1)S(1)} %copy-done, bf16[256,8192]{1,0:T(8,128)(2,1)} %cot.1, f32[2,512,512]{2,1,0:T(8,128)} %bitcast.5, s32[320]{0:T(512)S(1)} %pad_add_fusion.table), custom_call_target="tpu_custom_call" | custom-call | tf_op jit(solution)/shard_map/pallas_call | solution.py:401
  122.9 0.8 copy.8
  123.7 1.3 %copy.9 = f32[1,1,2,512,512]{4,3,2,1,0:T(8,128)} copy(f32[1,1,2,512,512]{4,3,2,1,0:T(8,128)S(1)} %bitcast.4) | data formatting | bytes 4194304
Async XLA Ops:
  2.4 1.6 %copy-start = (bf16[256,4096]{1,0:T(8,128)(2,1)S(1)}, bf16[256,4096]{1,0:T(8,128)(2,1)}, u32[]{:S(2)}) copy-start(bf16[256,4096]{1,0:T(8,128)(2,1)} %act.1) | copy-start | bytes 6291460

commit v2 on v1

v2 whole, which is shorter than its diff:
```python
import jax
import jax.numpy as jnp
from jax import lax
from jax.experimental import pallas as pl
from jax.experimental.pallas import tpu as pltpu
from jax.sharding import PartitionSpec as P

B = 512
Q = 128
ABOVE = [(0, 1), (0, 2), (0, 3), (1, 2), (1, 3), (2, 3)]
PIECE = 17
f32 = jnp.float32
bf16 = jnp.bfloat16


def split(x):
    hi = x.astype(bf16)
    return hi, (x - hi.astype(f32)).astype(bf16)


def dot(a, b, dims=((1,), (0,))):
    return lax.dot_general(a, b, (dims, ((), ())), preferred_element_type=f32)


def dot3(ah, al, bh, bl, dims=((1,), (0,))):
    return dot(ah, bh, dims) + (dot(ah, bl, dims) + dot(al, bh, dims))


def grid_ids(shape):
    return (
        lax.broadcasted_iota(jnp.int32, shape, 0),
        lax.broadcasted_iota(jnp.int32, shape, 1),
    )


def pack(read, write, write_extra):
    row, col = grid_ids((Q, Q))
    for n, (bi, bj) in enumerate(ABOVE):
        write(n, read(bi, bj))
    for pair in (0, 1):
        second = read(2 * pair + 1, 2 * pair + 1)
        write(6 + pair, jnp.where(row <= col, read(2 * pair, 2 * pair), second))
        write_extra(pair, jnp.sum(jnp.where(row == col, second, 0.0), axis=0, keepdims=True))


def unpack(packed, put):
    row, col = grid_ids((Q, Q))

    def block(n):
        return packed[pl.ds(8 * n, 8), pl.ds(0, 16), :].reshape(Q, Q)

    for n, (bi, bj) in enumerate(ABOVE):
        value = block(n)
        put(bi, bj, value)
        put(bj, bi, value.T)
    for pair in (0, 1):
        value = block(6 + pair)
        flipped = value.T
        extra = packed[pair, pl.ds(16, 1), :]
        put(2 * pair, 2 * pair, jnp.where(row <= col, value, flipped))
        put(
            2 * pair + 1,
            2 * pair + 1,
            jnp.where(row > col, value, jnp.where(row < col, flipped, extra)),
        )


def kernel(
    act, cot, owner_col, hist, prec, newh,
    act_own, act_part, cot_own, zact, zcot, act_full, cot_full,
    hv, hpk, hrecv, hsend, hfin, fpk, frecv, fsend, ffin,
    gtmp, gp, fbuf, xs, mats, pbuf, pfin, vtable, table,
    lsem, zsem, asem, osem, isem, csem, h1sem, h2sem, f1sem, f2sem, gsem, xsem, psend, precv,
):
    k = lax.axis_index("dp")
    mp = lax.axis_index("mp")
    s = lax.rem(mp, 2)
    chip = lax.div(mp, 2)
    zl = lax.rem(chip, 2)
    c = lax.div(mp, 4)
    x = lax.div(mp, 16)
    y = lax.rem(c, 4)
    w = lax.rem(mp, 4)
    par = lax.rem(k, 2)
    j = lax.div(k, 2)
    k1 = k + 1 - 2 * par
    k2 = lax.rem(k + 2, 4)
    k3 = lax.rem(k1 + 2, 4)
    mp1 = mp + 1 - 2 * s
    mp2 = mp + 2 - 4 * zl
    main = s == par

    def remote(src, dst, send, recv, dp_to, mp_to):
        return pltpu.make_async_remote_copy(
            src_ref=src, dst_ref=dst, send_sem=send, recv_sem=recv,
            device_id=(dp_to, mp_to), device_id_type=pl.DeviceIdType.MESH,
        )

    def wait_bytes(view, sem):
        pltpu.make_async_copy(view, view, sem).wait()

    barrier = pltpu.get_barrier_semaphore()

    def greet(dp_to, mp_to):
        pl.semaphore_signal(
            barrier, inc=1, device_id=(dp_to, mp_to), device_id_type=pl.DeviceIdType.MESH
        )

    def greet_beyond(step, _):
        greet(k1, lax.rem(mp + step, 64))
        return 0

    def greet_group(step, _):
        greet(k, lax.rem(mp + step, 64))
        return 0

    lax.fori_loop(0, 64, greet_beyond, 0)
    lax.fori_loop(1, 64, greet_group, 0)
    for dp_to, mp_to in ((k2, mp), (k3, mp), (k2, mp1), (k3, mp1), (k3, mp2)):
        greet(dp_to, mp_to)

    loads = []
    for jj in (0, 1):
        band = (4 * zl + 2 * s + jj) * B
        loads.append(
            pltpu.make_async_copy(
                act.at[pl.ds(c * 16, 16), pl.ds(band, B)], act_part.at[jj], lsem.at[3 + jj]
            )
        )
    loads.append(pltpu.make_async_copy(cot.at[:, pl.ds(c * B, B)], cot_own, lsem.at[2]))
    load_act = pltpu.make_async_copy(
        act.at[:, pl.ds((4 * zl + 2 * s + j) * B, B)], act_own, lsem.at[1]
    )
    load_hist = pltpu.make_async_copy(hist, hv, lsem.at[0])
    for copy in loads:
        copy.start()
    load_hist.start()
    load_act.start()
    for copy in loads:
        copy.wait()
    zact[...] = act_part[...].astype(f32).reshape(2, 2, 8, B)
    zcot[...] = cot_own[pl.ds(pl.multiple_of(s * 128, 128), 128), :].astype(f32).reshape(2, 64, B)
    own_col = jnp.broadcast_to(owner_col[...], (64, 128))
    own_row = jnp.transpose(own_col)[0:64, :]
    row, col = grid_ids((64, 64))
    same = own_col[:, 0:64] == own_row
    one = jnp.ones((64, 64), jnp.int32)
    zero = jnp.zeros((64, 64), jnp.int32)
    rank_col = jnp.sum(jnp.where(same & (col < row), one, zero), axis=1, keepdims=True)
    rank_row = jnp.sum(jnp.where(same & (row < col), one, zero), axis=0, keepdims=True)
    pick_row = 2 * own_row[0:1, :] + rank_row
    pick_col = 2 * owner_col[...] + rank_col
    row, col = grid_ids((64, 128))
    hit = pick_col == col
    vtable[0:1, 0:64] = pick_row
    vtable[0:1, 64:128] = pick_row
    vtable[1:2, :] = jnp.sum(jnp.where(hit, row, 0), axis=0, keepdims=True)
    vtable[2:3, :] = jnp.sum(jnp.where(hit, 1, 0), axis=0, keepdims=True)
    vtable[3:8, :] = jnp.zeros((5, 128), jnp.int32)
    load_table = pltpu.make_async_copy(vtable, table, lsem.at[5])
    load_table.start()
    load_hist.wait()
    for r in (0, 1):

        def write(n, value, r=r):
            hpk[r, pl.ds(8 * n, 8), pl.ds(0, 16), :] = value.reshape(8, 16, Q)

        def write_extra(pair, value, r=r):
            for p in range(pair, 64, 2):
                hpk[r, p, pl.ds(16, 1), :] = value

        pack(lambda bi, bj, r=r: hv[r, pl.ds(bi * Q, Q), pl.ds(bj * Q, Q)], write, write_extra)
    pl.semaphore_wait(barrier, 132)

    for e in (1, 2, 3):
        to = lax.rem(k + e, 4)
        remote(
            zact.at[lax.div(to, 2)], act_full.at[3 - e, x, y], zsem.at[0], zsem.at[1], to, mp
        ).start()

    def cot_rows(e, half):
        return cot_full.at[e, pl.ds(pl.multiple_of(s * 128 + half * 64, 64), 64), :]

    out_dp = lax.rem(k + 3 + 2 * zl, 4)
    e_out, e_in = 2 * zl, 2 - 2 * zl
    first, second = 1 - zl, zl
    outs = [
        remote(zcot.at[first], cot_rows(e_out, first), osem.at[0], osem.at[3], out_dp, mp2),
        remote(zcot.at[second], cot_rows(e_out, second), osem.at[1], osem.at[4], out_dp, mp2),
        remote(cot_rows(e_out, first), cot_rows(1, first), osem.at[2], osem.at[5], out_dp, mp2),
    ]
    inward = [cot_rows(e_in, second), cot_rows(e_in, first), cot_rows(1, second)]
    ins = [
        remote(view, view, isem.at[n], isem.at[3 + n], k, mp2) for n, view in enumerate(inward)
    ]

    def swap(view):
        remote(view, view, csem.at[0], csem.at[1], k, mp1).start()

    outs[0].start()
    outs[1].start()

    def spread(src_of, dst, send, recv):
        def to_device(step, _):
            to = lax.rem(mp + step, 64)
            remote(src_of(to), dst, send, recv, k, to).start()
            return 0

        lax.fori_loop(1, 64, to_device, 0)
        pltpu.make_async_copy(src_of(mp), dst, recv).start()

    spread(
        lambda to: hpk.at[:, to, pl.ds(0, PIECE), :],
        hrecv.at[pl.ds(2 * mp, 2), pl.ds(0, PIECE), :],
        h1sem.at[0],
        h1sem.at[1],
    )

    wait_bytes(act_full.at[:, x, y], zsem.at[1])
    for d in (1, 2, 3):
        to_x = lax.rem(mp + 16 * d, 64)
        to_y = 16 * x + lax.rem(4 * y + 4 * d, 16) + w
        view = act_full.at[:, x, y, 0]
        remote(view, view, asem.at[0], asem.at[1], k, to_x).start()
        view = act_full.at[:, x, y, 1]
        remote(view, view, asem.at[2], asem.at[3], k, to_y).start()
    outs[0].wait_recv()
    ins[0].start()
    swap(inward[0])
    wait_bytes(act_full.at[:, pl.ds(0, 3), 0, 0], asem.at[1])
    wait_bytes(act_full.at[:, pl.ds(0, 3), 0, 0], asem.at[3])
    for d in (1, 2, 3):
        to_x = lax.rem(mp + 16 * d, 64)
        to_y = 16 * x + lax.rem(4 * y + 4 * d, 16) + w
        view = act_full.at[:, :, y, 0]
        remote(view, view, asem.at[4], asem.at[5], k, to_y).start()
        view = act_full.at[:, x, :, 1]
        remote(view, view, asem.at[6], asem.at[7], k, to_x).start()
    outs[1].wait_recv()
    ins[1].start()
    swap(inward[1])
    ins[0].wait_recv()
    outs[2].start()
    swap(cot_rows(e_out, first))
    load_act.wait()
    down = ((0,), (0,))
    for half in (0, 1):
        rows = pl.ds(half * 256, 256)
        gtmp[rows, :] = dot(act_own[:, rows], cot_own[...], down)
    outs[2].wait_recv()
    ins[2].start()
    swap(inward[2])
    ins[1].wait_recv()
    swap(cot_rows(e_out, second))
    ins[2].wait_recv()
    swap(cot_rows(1, first))

    load_table.wait()
    wait_bytes(hrecv.at[:, pl.ds(0, PIECE), :], h1sem.at[1])

    def choose(g, _):
        hsend[g, pl.ds(0, PIECE), :] = hrecv[table[0, g], pl.ds(0, PIECE), :]
        return 0

    lax.fori_loop(0, 64, choose, 0)
    mine = hfin.at[mp, pl.ds(0, PIECE), :]

    def chosen(g):
        return hsend.at[g, pl.ds(0, PIECE), :]

    def to_chip(step, _):
        to = 2 * lax.rem(chip + step, 32)
        remote(chosen(to + par), mine, h2sem.at[0], h2sem.at[1], k, to + par).start()
        remote(chosen(to + 1 - par), mine, h2sem.at[0], h2sem.at[1], k1, to + par).start()
        return 0

    lax.fori_loop(1, 32, to_chip, 0)
    here = 2 * chip
    remote(chosen(here + 1 - par), mine, h2sem.at[0], h2sem.at[1], k1, here + par).start()

    @pl.when(main)
    def _():
        pltpu.make_async_copy(chosen(here + par), mine, h2sem.at[1]).start()

    @pl.when(jnp.logical_not(main))
    def _():
        remote(chosen(here + par), mine, h2sem.at[0], h2sem.at[1], k, mp1).start()

    wait_bytes(act_full.at[:, pl.ds(0, 3), :, 0], asem.at[5])
    wait_bytes(act_full.at[:, pl.ds(0, 3), :, 0], asem.at[7])
    wait_bytes(cot_full.at[:, pl.ds(0, 128), :], csem.at[1])
    for half in (0, 1):
        rows = pl.ds(half * 256, 256)
        total = gtmp[rows, :]
        for e in range(3):
            left = act_full[e, :, :, :, :, rows].reshape(256, 256).astype(bf16)
            total += dot(left, cot_full[e].astype(bf16), down)
        gtmp[rows, :] = total
    send_g = remote(gtmp, gp, gsem.at[0], gsem.at[1], k, mp1)

    @pl.when(main)
    def _():
        send_g.start()
        gp[...] = gtmp[...]

    gh, gl = mats.at[0], mats.at[1]

    def fresh(g_ref, side):
        hi, lo = split(g_ref[...])
        gh[...] = hi
        gl[...] = lo
        for which, dims in ((0, ((1,), (1,))), (1, ((0,), (0,)))):

            @pl.when(side == which)
            def _(dims=dims):
                fbuf[...] = dot3(gh[...], gl[...], gh[...], gl[...], dims) * (1.0 / B)

    fresh(gtmp, par)

    def write_f(n, value):
        fpk[pl.ds(8 * n, 8), pl.ds(0, 16), :] = value.reshape(8, 16, Q)

    def write_f_extra(pair, value):
        for p in range(pair, 64, 2):
            fpk[p, pl.ds(16, 1), :] = value

    pack(lambda bi, bj: fbuf[pl.ds(bi * Q, Q), pl.ds(bj * Q, Q)], write_f, write_f_extra)
    spread(
        lambda to: fpk.at[to, pl.ds(0, PIECE), :],
        frecv.at[mp, pl.ds(0, PIECE), :],
        f1sem.at[0],
        f1sem.at[1],
    )

    @pl.when(jnp.logical_not(main))
    def _():
        send_g.wait_recv()
        fresh(gp, s)

    wait_bytes(hfin.at[:, pl.ds(0, PIECE), :], h2sem.at[1])

    def merge(bi, bj, value):
        at = (pl.ds(bi * Q, Q), pl.ds(bj * Q, Q))
        fbuf[at] = 0.8 * value + 0.2 * fbuf[at]

    unpack(hfin, merge)
    square = jnp.sum(fbuf[...] * fbuf[...], axis=0, keepdims=True)
    norm = jnp.sqrt(jnp.sum(square, axis=1, keepdims=True)) + 1e-06
    scale = 2.5 / norm
    root_scale = jnp.sqrt(jnp.sqrt(scale))

    def store(slot, rows, value):
        hi, lo = split(value)
        mats[slot, rows, :] = hi
        mats[slot + 1, rows, :] = lo

    def factor(rows, start, value):
        row = start + lax.broadcasted_iota(jnp.int32, value.shape, 0)
        col = lax.broadcasted_iota(jnp.int32, value.shape, 1)
        return jnp.where(row == col, 1.25, 0.0) - 0.25 * value

    def product(a, b, after):
        for start in (0, 256):
            rows = pl.ds(start, 256)
            after(
                rows,
                start,
                dot3(mats[a, rows, :], mats[a + 1, rows, :], mats[b], mats[b + 1]),
            )

    MG, MQ, MS, MF, MM, MX, MR = 0, 2, 4, 6, 8, 10, 12
    for start in (0, 256):
        rows = pl.ds(start, 256)
        value = fbuf[rows, :] * scale
        store(MM, rows, value)
        store(MX, rows, factor(rows, start, value))
    product(MX, MX, lambda rows, start, value: store(MS, rows, value))
    product(MS, MS, lambda rows, start, value: store(MF, rows, value))

    wait_bytes(frecv.at[:, pl.ds(0, PIECE), :], f1sem.at[1])

    def choose_fresh(o, _):
        for r in (0, 1):
            fsend[o, r, pl.ds(0, PIECE), :] = frecv[table[1, 2 * o + r], pl.ds(0, PIECE), :]
        return 0

    lax.fori_loop(0, 64, choose_fresh, 0)
    spread(
        lambda to: fsend.at[to, :, pl.ds(0, PIECE), :],
        ffin.at[:, mp, pl.ds(0, PIECE), :],
        f2sem.at[0],
        f2sem.at[1],
    )

    def next_step(rows, start, value):
        store(MR, rows, value)
        store(MQ, rows, factor(rows, start, value))

    product(MF, MM, next_step)
    product(MX, MQ, lambda rows, start, value: store(MM, rows, value))
    product(MQ, MQ, lambda rows, start, value: store(MS, rows, value))
    product(MS, MS, lambda rows, start, value: store(MF, rows, value))
    product(
        MF, MR, lambda rows, start, value: store(MQ, rows, factor(rows, start, value))
    )

    def last(rows, start, value):
        xs[s, rows, :] = value * root_scale

    product(MM, MQ, last)
    send_x = remote(xs.at[s], xs.at[s], xsem.at[0], xsem.at[1], k, mp1)
    send_x.start()
    store(MG, pl.ds(0, B), gp[...])
    send_x.wait_recv()

    store(MX, pl.ds(0, B), xs[1])
    copies = []
    for e in (0, 1):
        to = s + 2 * e
        hi, lo = split(xs[0, pl.ds(pl.multiple_of(to * Q, Q), Q), :])
        hi, lo = split(dot3(hi, lo, mats[MG], mats[MG + 1]))
        pbuf[e] = dot3(hi, lo, mats[MX], mats[MX + 1])
        copy = remote(pbuf.at[e], pfin.at[j], psend.at[e], precv.at[j], to, 2 * chip + par)
        away = jnp.logical_not(jnp.logical_and(main, to == k))
        pl.when(away)(copy.start)

        @pl.when(jnp.logical_not(away))
        def _(e=e):
            pfin[j] = pbuf[e]

        copies.append((copy, away))

    wait_bytes(ffin.at[:, :, pl.ds(0, PIECE), :], f2sem.at[1])
    for r in (0, 1):
        used = table[2, 2 * mp + r] > 0

        def renew(bi, bj, value, r=r, used=used):
            at = (r, pl.ds(bi * Q, Q), pl.ds(bj * Q, Q))
            held = hv[at]
            hv[at] = jnp.where(used, 0.8 * held + 0.2 * value, held)

        unpack(ffin.at[r], renew)
    out_h = pltpu.make_async_copy(hv, newh, lsem.at[0])
    out_h.start()
    for jj in (0, 1):

        @pl.when(2 * jj + s != k)
        def _(jj=jj):
            wait_bytes(pfin.at[jj], precv.at[jj])

    out_p = pltpu.make_async_copy(pfin, prec, lsem.at[1])
    out_p.start()

    wait_bytes(act_full.at[:, x, y], zsem.at[0])
    for n in (0, 2):
        wait_bytes(act_full.at[:, pl.ds(0, 3), 0, 0], asem.at[n])
    for n in (4, 6):
        wait_bytes(act_full.at[:, pl.ds(0, 3), :, 0], asem.at[n])
    for copy in outs + ins:
        copy.wait_send()
    wait_bytes(cot_full.at[:, pl.ds(0, 128), :], csem.at[0])
    wait_bytes(hpk.at[:, pl.ds(0, 63), pl.ds(0, PIECE), :], h1sem.at[0])
    wait_bytes(fpk.at[pl.ds(0, 63), pl.ds(0, PIECE), :], f1sem.at[0])
    wait_bytes(fsend.at[pl.ds(0, 63), :, pl.ds(0, PIECE), :], f2sem.at[0])
    wait_bytes(hsend.at[pl.ds(0, 63), pl.ds(0, PIECE), :], h2sem.at[0])

    @pl.when(jnp.logical_not(main))
    def _():
        wait_bytes(hsend.at[0, pl.ds(0, PIECE), :], h2sem.at[0])

    pl.when(main)(send_g.wait_send)
    send_x.wait_send()
    for copy, away in copies:
        pl.when(away)(copy.wait_send)
    out_h.wait()
    out_p.wait()


def body(activations, cotangent, owners, history):
    anywhere = pl.BlockSpec(memory_space=pl.ANY)
    dma = pltpu.SemaphoreType.DMA
    prec, newh = pl.pallas_call(
        kernel,
        out_shape=[
            jax.ShapeDtypeStruct((2, 128, B), f32),
            jax.ShapeDtypeStruct((2, B, B), f32),
        ],
        in_specs=[anywhere, anywhere, pl.BlockSpec(memory_space=pltpu.VMEM), anywhere],
        out_specs=[anywhere, anywhere],
        scratch_shapes=[
            pltpu.VMEM((256, B), bf16),
            pltpu.VMEM((2, 16, B), bf16),
            pltpu.VMEM((256, B), bf16),
            pltpu.VMEM((2, 2, 8, B), f32),
            pltpu.VMEM((2, 64, B), f32),
            pltpu.VMEM((3, 4, 4, 2, 8, B), f32),
            pltpu.VMEM((3, 256, B), f32),
            pltpu.VMEM((2, B, B), f32),
            pltpu.VMEM((2, 64, 24, Q), f32),
            pltpu.VMEM((128, 24, Q), f32),
            pltpu.VMEM((64, 24, Q), f32),
            pltpu.VMEM((64, 24, Q), f32),
            pltpu.VMEM((64, 24, Q), f32),
            pltpu.VMEM((64, 24, Q), f32),
            pltpu.VMEM((64, 2, 24, Q), f32),
            pltpu.VMEM((2, 64, 24, Q), f32),
            pltpu.VMEM((B, B), f32),
            pltpu.VMEM((B, B), f32),
            pltpu.VMEM((B, B), f32),
            pltpu.VMEM((2, B, B), f32),
            pltpu.VMEM((14, B, B), bf16),
            pltpu.VMEM((2, 128, B), f32),
            pltpu.VMEM((2, 128, B), f32),
            pltpu.VMEM((8, 128), jnp.int32),
            pltpu.SMEM((8, 128), jnp.int32),
            dma((6,)),
            dma((2,)),
            dma((8,)),
            dma((6,)),
            dma((6,)),
            dma((2,)),
            dma((2,)),
            dma((2,)),
            dma((2,)),
            dma((2,)),
            dma((2,)),
            dma((2,)),
            dma((2,)),
            dma((2,)),
        ],
        compiler_params=pltpu.CompilerParams(
            collective_id=0, has_side_effects=True, vmem_limit_bytes=48 * 1024 * 1024
        ),
    )(activations, cotangent, owners[0], history[0, 0])
    return prec, newh[None, None]


def solution(mesh):
    return jax.shard_map(
        body,
        mesh=mesh,
        in_specs=(
            P("dp", None),
            P("dp", None),
            P("dp", None, None),
            P("dp", "mp", None, None, None),
        ),
        out_specs=(P("mp", "dp", None), P("dp", "mp", None, None, None)),
        check_vma=False,
    )
```

time: 125 us -> 90.2 us (0.72)
  the two profiles are of different devices: /device:TPU:5 before, /device:TPU:4 now
where the time goes in v2:
time: 90.2 us; the launch traced here: 90.1 us
  Pallas kernels  85 us (94%)
  local copies, waits for them, and re-layouts  4.45 us (5%)
    pallas_call x1, Pallas kernels, body(): pl.pallas_call(kernel, out_shape=[jax.ShapeDtypeStruct((2, 128, B), f32),...  85 us
    unnamed x4, local copies, waits for them, and re-layouts  3.7 us

profile of v2, /device:TPU:4, one launch (start us, length us, event | category | flops | bytes accessed | tf_op | source)
XLA Modules:
  0.0 90.1 jit_solution(2878285855606897993)
XLA Ops:
  0.6 0.7 copy.6.owner_col
  1.4 0.0 copy-start
  1.4 1.6 %copy-done = bf16[256,4096]{1,0:T(8,128)(2,1)S(1)} copy-done((bf16[256,4096]{1,0:T(8,128)(2,1)S(1)}, bf16[256,4096]{1,0:T(8,128)(2,1)}, u32[]{:S(2)}) %copy-start) | copy-done | bytes 2097176
  3.0 85.0 %shard_map.59 = (f32[2,128,512]{2,1,0:T(8,128)S(1)}, f32[2,512,512]{2,1,0:T(8,128)S(1)}) custom-call(bf16[256,4096]{1,0:T(8,128)(2,1)S(1)} %copy-done, bf16[256,8192]{1,0:T(8,128)(2,1)} %cot.1, s32[64,1]{1,0:T(8,128)S(1)} %copy.6.owner_col, f32[2,512,512]{2,1,0:T(8,128)} %bitcast.4), custom_call_target="tpu_custom_call" | custom-call | tf_op jit(solution)/shard_map/pallas_call | solution.py:482
  87.9 0.8 copy.9
  88.7 1.3 %copy.10 = f32[1,1,2,512,512]{4,3,2,1,0:T(8,128)} copy(f32[1,1,2,512,512]{4,3,2,1,0:T(8,128)S(1)} %bitcast.3) | data formatting | bytes 4194304
Async XLA Ops:
  1.4 1.6 %copy-start = (bf16[256,4096]{1,0:T(8,128)(2,1)S(1)}, bf16[256,4096]{1,0:T(8,128)(2,1)}, u32[]{:S(2)}) copy-start(bf16[256,4096]{1,0:T(8,128)(2,1)} %act.1) | copy-start | bytes 6291460

commit v3 on v2

--- a/solution.py
+++ b/solution.py
@@ -47,7 +47,7 @@
     row, col = grid_ids((Q, Q))
 
     def block(n):
-        return packed[pl.ds(8 * n, 8), pl.ds(0, 16), :].reshape(Q, Q)
+        return packed[pl.ds(4 * n, 4), :, pl.ds(0, 16), :].reshape(Q, Q)
 
     for n, (bi, bj) in enumerate(ABOVE):
         value = block(n)
@@ -56,7 +56,7 @@
     for pair in (0, 1):
         value = block(6 + pair)
         flipped = value.T
-        extra = packed[pair, pl.ds(16, 1), :]
+        extra = packed[0, pair, pl.ds(16, 1), :]
         put(2 * pair, 2 * pair, jnp.where(row <= col, value, flipped))
         put(
             2 * pair + 1,
@@ -66,11 +66,11 @@
 
 
 def kernel(
-    act, cot, owner_col, hist, prec, newh,
+    act, cot, owner_row, hist, prec, newh,
     act_own, act_part, cot_own, zact, zcot, act_full, cot_full,
     hv, hpk, hrecv, hsend, hfin, fpk, frecv, fsend, ffin,
     gtmp, gp, fbuf, xs, mats, pbuf, pfin, vtable, table,
-    lsem, zsem, asem, osem, isem, csem, h1sem, h2sem, f1sem, f2sem, gsem, xsem, psend, precv,
+    lsem, zsem, asem, osem, isem, csem, h1sem, h2sem, f1sem, fwsem, f2sem, gsem, xsem, psend, precv,
 ):
     k = lax.axis_index("dp")
     mp = lax.axis_index("mp")
@@ -99,26 +99,6 @@
     def wait_bytes(view, sem):
         pltpu.make_async_copy(view, view, sem).wait()
 
-    barrier = pltpu.get_barrier_semaphore()
-
-    def greet(dp_to, mp_to):
-        pl.semaphore_signal(
-            barrier, inc=1, device_id=(dp_to, mp_to), device_id_type=pl.DeviceIdType.MESH
-        )
-
-    def greet_beyond(step, _):
-        greet(k1, lax.rem(mp + step, 64))
-        return 0
-
-    def greet_group(step, _):
-        greet(k, lax.rem(mp + step, 64))
-        return 0
-
-    lax.fori_loop(0, 64, greet_beyond, 0)
-    lax.fori_loop(1, 64, greet_group, 0)
-    for dp_to, mp_to in ((k2, mp), (k3, mp), (k2, mp1), (k3, mp1), (k3, mp2)):
-        greet(dp_to, mp_to)
-
     loads = []
     for jj in (0, 1):
         band = (4 * zl + 2 * s + jj) * B
@@ -136,12 +116,33 @@
         copy.start()
     load_hist.start()
     load_act.start()
+    barrier = pltpu.get_barrier_semaphore()
+
+    def greet(dp_to, mp_to):
+        pl.semaphore_signal(
+            barrier, inc=1, device_id=(dp_to, mp_to), device_id_type=pl.DeviceIdType.MESH
+        )
+
+    def greet_beyond(step, _):
+        greet(k1, lax.rem(mp + step, 64))
+        return 0
+
+    def greet_group(step, _):
+        greet(k, lax.rem(mp + step, 64))
+        return 0
+
+    lax.fori_loop(0, 64, greet_beyond, 0)
+    lax.fori_loop(1, 64, greet_group, 0)
+    for dp_to, mp_to in ((k2, mp), (k3, mp), (k2, mp1), (k3, mp1), (k3, mp2)):
+        greet(dp_to, mp_to)
+
     for copy in loads:
         copy.wait()
     zact[...] = act_part[...].astype(f32).reshape(2, 2, 8, B)
     zcot[...] = cot_own[pl.ds(pl.multiple_of(s * 128, 128), 128), :].astype(f32).reshape(2, 64, B)
-    own_col = jnp.broadcast_to(owner_col[...], (64, 128))
-    own_row = jnp.transpose(own_col)[0:64, :]
+    own_row = jnp.broadcast_to(owner_row[...], (128, 64))
+    own_col = jnp.transpose(own_row)
+    own_row = own_row[0:64, :]
     row, col = grid_ids((64, 64))
     same = own_col[:, 0:64] == own_row
     one = jnp.ones((64, 64), jnp.int32)
@@ -149,12 +150,13 @@
     rank_col = jnp.sum(jnp.where(same & (col < row), one, zero), axis=1, keepdims=True)
     rank_row = jnp.sum(jnp.where(same & (row < col), one, zero), axis=0, keepdims=True)
     pick_row = 2 * own_row[0:1, :] + rank_row
-    pick_col = 2 * owner_col[...] + rank_col
+    pick_col = 2 * own_col[:, 0:1] + rank_col
     row, col = grid_ids((64, 128))
     hit = pick_col == col
+    place = (row & 2) * 16 + (row >> 2) * 2 + (row & 1)
     vtable[0:1, 0:64] = pick_row
     vtable[0:1, 64:128] = pick_row
-    vtable[1:2, :] = jnp.sum(jnp.where(hit, row, 0), axis=0, keepdims=True)
+    vtable[1:2, :] = jnp.sum(jnp.where(hit, place, 0), axis=0, keepdims=True)
     vtable[2:3, :] = jnp.sum(jnp.where(hit, 1, 0), axis=0, keepdims=True)
     vtable[3:8, :] = jnp.zeros((5, 128), jnp.int32)
     load_table = pltpu.make_async_copy(vtable, table, lsem.at[5])
@@ -263,7 +265,7 @@
         return 0
 
     lax.fori_loop(0, 64, choose, 0)
-    mine = hfin.at[mp, pl.ds(0, PIECE), :]
+    mine = hfin.at[chip, s, pl.ds(0, PIECE), :]
 
     def chosen(g):
         return hsend.at[g, pl.ds(0, PIECE), :]
@@ -318,18 +320,30 @@
     fresh(gtmp, par)
 
     def write_f(n, value):
-        fpk[pl.ds(8 * n, 8), pl.ds(0, 16), :] = value.reshape(8, 16, Q)
+        fpk[pl.ds(4 * n, 4), :, pl.ds(0, 16), :] = value.reshape(4, 2, 16, Q)
 
     def write_f_extra(pair, value):
-        for p in range(pair, 64, 2):
-            fpk[p, pl.ds(16, 1), :] = value
+        for p in range(32):
+            fpk[p, pair, pl.ds(16, 1), :] = value
 
     pack(lambda bi, bj: fbuf[pl.ds(bi * Q, Q), pl.ds(bj * Q, Q)], write_f, write_f_extra)
-    spread(
-        lambda to: fpk.at[to, pl.ds(0, PIECE), :],
-        frecv.at[mp, pl.ds(0, PIECE), :],
+    flat = 2 * c + s
+
+    def spread_plane(src_of, dst, send, recv):
+        def to_device(step, _):
+            to = lax.rem(flat + step, 32)
+            to_mp = 4 * lax.div(to, 2) + 2 * zl + lax.rem(to, 2)
+            remote(src_of(to), dst, send, recv, k, to_mp).start()
+            return 0
+
+        lax.fori_loop(1, 32, to_device, 0)
+        pltpu.make_async_copy(src_of(flat), dst, recv).start()
+
+    spread_plane(
+        lambda to: fpk.at[to, :, pl.ds(0, PIECE), :],
+        frecv.at[32 * zl + flat, :, pl.ds(0, PIECE), :],
         f1sem.at[0],
-        f1sem.at[1],
+        f1sem.at[1 + x],
     )
 
     @pl.when(jnp.logical_not(main))
@@ -337,7 +351,13 @@
         send_g.wait_recv()
         fresh(gp, s)
 
-    wait_bytes(hfin.at[:, pl.ds(0, PIECE), :], h2sem.at[1])
+    for d in (0, 1, 3, 2):
+        from_x = lax.rem(x + d, 4)
+        view = frecv.at[pl.ds(32 * zl + 8 * from_x, 8), :, pl.ds(0, PIECE), :]
+        wait_bytes(view, f1sem.at[1 + from_x])
+        remote(view, view, fwsem.at[0], fwsem.at[1], k, mp2).start()
+
+    wait_bytes(hfin.at[:, :, pl.ds(0, PIECE), :], h2sem.at[1])
 
     def merge(bi, bj, value):
         at = (pl.ds(bi * Q, Q), pl.ds(bj * Q, Q))
@@ -377,21 +397,6 @@
     product(MX, MX, lambda rows, start, value: store(MS, rows, value))
     product(MS, MS, lambda rows, start, value: store(MF, rows, value))
 
-    wait_bytes(frecv.at[:, pl.ds(0, PIECE), :], f1sem.at[1])
-
-    def choose_fresh(o, _):
-        for r in (0, 1):
-            fsend[o, r, pl.ds(0, PIECE), :] = frecv[table[1, 2 * o + r], pl.ds(0, PIECE), :]
-        return 0
-
-    lax.fori_loop(0, 64, choose_fresh, 0)
-    spread(
-        lambda to: fsend.at[to, :, pl.ds(0, PIECE), :],
-        ffin.at[:, mp, pl.ds(0, PIECE), :],
-        f2sem.at[0],
-        f2sem.at[1],
-    )
-
     def next_step(rows, start, value):
         store(MR, rows, value)
         store(MQ, rows, factor(rows, start, value))
@@ -404,33 +409,56 @@
         MF, MR, lambda rows, start, value: store(MQ, rows, factor(rows, start, value))
     )
 
+    sends_x = []
+
     def last(rows, start, value):
         xs[s, rows, :] = value * root_scale
+        view = xs.at[s, rows, :]
+        n = start // 256
+        sends_x.append(remote(view, view, xsem.at[n], xsem.at[2 + n], k, mp1))
+        sends_x[-1].start()
 
     product(MM, MQ, last)
-    send_x = remote(xs.at[s], xs.at[s], xsem.at[0], xsem.at[1], k, mp1)
-    send_x.start()
     store(MG, pl.ds(0, B), gp[...])
-    send_x.wait_recv()
+
+    wait_bytes(frecv.at[pl.ds(32 - 32 * zl, 32), :, pl.ds(0, PIECE), :], fwsem.at[1])
+
+    def choose_fresh(o, _):
+        owner = 4 * lax.div(o, 2) + 2 * zl + lax.rem(o, 2)
+        for r in (0, 1):
+            g = table[1, 2 * owner + r]
+            fsend[o, r, :, pl.ds(0, PIECE), :] = frecv[g, :, pl.ds(0, PIECE), :]
+        return 0
+
+    lax.fori_loop(0, 32, choose_fresh, 0)
+    spread_plane(
+        lambda to: fsend.at[to, :, :, pl.ds(0, PIECE), :],
+        ffin.at[:, flat, :, pl.ds(0, PIECE), :],
+        f2sem.at[0],
+        f2sem.at[1],
+    )
+    for copy in sends_x:
+        copy.wait_recv()
 
     store(MX, pl.ds(0, B), xs[1])
     copies = []
-    for e in (0, 1):
-        to = s + 2 * e
+    for e, to in enumerate((jnp.where(main, k2, k1), jnp.where(main, k, k3))):
         hi, lo = split(xs[0, pl.ds(pl.multiple_of(to * Q, Q), Q), :])
         hi, lo = split(dot3(hi, lo, mats[MG], mats[MG + 1]))
         pbuf[e] = dot3(hi, lo, mats[MX], mats[MX + 1])
-        copy = remote(pbuf.at[e], pfin.at[j], psend.at[e], precv.at[j], to, 2 * chip + par)
-        away = jnp.logical_not(jnp.logical_and(main, to == k))
-        pl.when(away)(copy.start)
-
-        @pl.when(jnp.logical_not(away))
-        def _(e=e):
-            pfin[j] = pbuf[e]
-
-        copies.append((copy, away))
-
-    wait_bytes(ffin.at[:, :, pl.ds(0, PIECE), :], f2sem.at[1])
+        copies.append(
+            remote(pbuf.at[e], pfin.at[j], psend.at[e], precv.at[j], to, 2 * chip + par)
+        )
+        if e == 0:
+            copies[0].start()
+
+    @pl.when(main)
+    def _():
+        pfin[j] = pbuf[1]
+
+    pl.when(jnp.logical_not(main))(copies[1].start)
+
+    wait_bytes(ffin.at[:, :, :, pl.ds(0, PIECE), :], f2sem.at[1])
     for r in (0, 1):
         used = table[2, 2 * mp + r] > 0
 
@@ -460,8 +488,9 @@
         copy.wait_send()
     wait_bytes(cot_full.at[:, pl.ds(0, 128), :], csem.at[0])
     wait_bytes(hpk.at[:, pl.ds(0, 63), pl.ds(0, PIECE), :], h1sem.at[0])
-    wait_bytes(fpk.at[pl.ds(0, 63), pl.ds(0, PIECE), :], f1sem.at[0])
-    wait_bytes(fsend.at[pl.ds(0, 63), :, pl.ds(0, PIECE), :], f2sem.at[0])
+    wait_bytes(fpk.at[pl.ds(0, 31), :, pl.ds(0, PIECE), :], f1sem.at[0])
+    wait_bytes(frecv.at[pl.ds(0, 32), :, pl.ds(0, PIECE), :], fwsem.at[0])
+    wait_bytes(fsend.at[pl.ds(0, 31), :, :, pl.ds(0, PIECE), :], f2sem.at[0])
     wait_bytes(hsend.at[pl.ds(0, 63), pl.ds(0, PIECE), :], h2sem.at[0])
 
     @pl.when(jnp.logical_not(main))
@@ -469,9 +498,10 @@
         wait_bytes(hsend.at[0, pl.ds(0, PIECE), :], h2sem.at[0])
 
     pl.when(main)(send_g.wait_send)
-    send_x.wait_send()
-    for copy, away in copies:
-        pl.when(away)(copy.wait_send)
+    for copy in sends_x:
+        copy.wait_send()
+    copies[0].wait_send()
+    pl.when(jnp.logical_not(main))(copies[1].wait_send)
     out_h.wait()
     out_p.wait()
 
@@ -499,11 +529,11 @@
             pltpu.VMEM((2, 64, 24, Q), f32),
             pltpu.VMEM((128, 24, Q), f32),
             pltpu.VMEM((64, 24, Q), f32),
-            pltpu.VMEM((64, 24, Q), f32),
-            pltpu.VMEM((64, 24, Q), f32),
-            pltpu.VMEM((64, 24, Q), f32),
+            pltpu.VMEM((32, 2, 24, Q), f32),
+            pltpu.VMEM((32, 2, 24, Q), f32),
             pltpu.VMEM((64, 2, 24, Q), f32),
-            pltpu.VMEM((2, 64, 24, Q), f32),
+            pltpu.VMEM((32, 2, 2, 24, Q), f32),
+            pltpu.VMEM((2, 32, 2, 24, Q), f32),
             pltpu.VMEM((B, B), f32),
             pltpu.VMEM((B, B), f32),
             pltpu.VMEM((B, B), f32),
@@ -521,17 +551,18 @@
             dma((2,)),
             dma((2,)),
             dma((2,)),
-            dma((2,)),
-            dma((2,)),
-            dma((2,)),
-            dma((2,)),
+            dma((5,)),
+            dma((2,)),
+            dma((2,)),
+            dma((2,)),
+            dma((4,)),
             dma((2,)),
             dma((2,)),
         ],
         compiler_params=pltpu.CompilerParams(
-            collective_id=0, has_side_effects=True, vmem_limit_bytes=48 * 1024 * 1024
+            collective_id=0, has_side_effects=True, vmem_limit_bytes=62 * 1024 * 1024
         ),
-    )(activations, cotangent, owners[0], history[0, 0])
+    )(activations, cotangent, owners.reshape(1, -1), history[0, 0])
     return prec, newh[None, None]
 
 

time: 90.2 us -> 95.4 us (1.058)
  the two profiles are of different devices: /device:TPU:4 before, /device:TPU:25 now
where the time goes in v3:
time: 95.4 us; the launch traced here: 95.2 us
  Pallas kernels  89.6 us (94%)
  local copies, waits for them, and re-layouts  4.95 us (5%)
    pallas_call x1, Pallas kernels, body(): pl.pallas_call(kernel, out_shape=[jax.ShapeDtypeStruct((2, 128, B), f32),...  89.6 us
    unnamed x2, local copies, waits for them, and re-layouts  4.95 us

profile of v3, /device:TPU:25, one launch (start us, length us, event | category | flops | bytes accessed | tf_op | source)
XLA Modules:
  0.0 95.2 jit_solution(3241836922922670386)
XLA Ops:
  0.6 89.6 %shard_map.59 = (f32[2,128,512]{2,1,0:T(8,128)}, f32[2,512,512]{2,1,0:T(8,128)}) custom-call(bf16[256,4096]{1,0:T(8,128)(2,1)} %act.1, bf16[256,8192]{1,0:T(8,128)(2,1)} %cot.1, s32[1,64]{1,0:T(1,128)} %bitcast.5, f32[2,512,512]{2,1,0:T(8,128)} %bitcast.4), custom_call_target="tpu_custom_call" | custom-call | tf_op jit(solution)/shard_map/pallas_call | solution.py:512
  90.2 1.9 %copy.8 = f32[2,128,512]{2,1,0:T(8,128)} copy(f32[2,128,512]{2,1,0:T(8,128)} %get-tuple-element.8) | data formatting | bytes 1048576
  92.1 3.1 %copy.9 = f32[1,1,2,512,512]{4,3,2,1,0:T(8,128)} copy(f32[1,1,2,512,512]{4,3,2,1,0:T(8,128)} %bitcast.3) | data formatting | bytes 4194304

commit v4 on v3

--- a/solution.py
+++ b/solution.py
@@ -47,7 +47,7 @@
     row, col = grid_ids((Q, Q))
 
     def block(n):
-        return packed[pl.ds(4 * n, 4), :, pl.ds(0, 16), :].reshape(Q, Q)
+        return packed[pl.ds(8 * n, 8), pl.ds(0, 16), :].reshape(Q, Q)
 
     for n, (bi, bj) in enumerate(ABOVE):
         value = block(n)
@@ -56,7 +56,7 @@
     for pair in (0, 1):
         value = block(6 + pair)
         flipped = value.T
-        extra = packed[0, pair, pl.ds(16, 1), :]
+        extra = packed[pair, pl.ds(16, 1), :]
         put(2 * pair, 2 * pair, jnp.where(row <= col, value, flipped))
         put(
             2 * pair + 1,
@@ -70,7 +70,7 @@
     act_own, act_part, cot_own, zact, zcot, act_full, cot_full,
     hv, hpk, hrecv, hsend, hfin, fpk, frecv, fsend, ffin,
     gtmp, gp, fbuf, xs, mats, pbuf, pfin, vtable, table,
-    lsem, zsem, asem, osem, isem, csem, h1sem, h2sem, f1sem, fwsem, f2sem, gsem, xsem, psend, precv,
+    lsem, zsem, asem, osem, isem, csem, h1sem, h2sem, f1sem, f2sem, gsem, xsem, psend, precv,
 ):
     k = lax.axis_index("dp")
     mp = lax.axis_index("mp")
@@ -153,10 +153,9 @@
     pick_col = 2 * own_col[:, 0:1] + rank_col
     row, col = grid_ids((64, 128))
     hit = pick_col == col
-    place = (row & 2) * 16 + (row >> 2) * 2 + (row & 1)
     vtable[0:1, 0:64] = pick_row
     vtable[0:1, 64:128] = pick_row
-    vtable[1:2, :] = jnp.sum(jnp.where(hit, place, 0), axis=0, keepdims=True)
+    vtable[1:2, :] = jnp.sum(jnp.where(hit, row, 0), axis=0, keepdims=True)
     vtable[2:3, :] = jnp.sum(jnp.where(hit, 1, 0), axis=0, keepdims=True)
     vtable[3:8, :] = jnp.zeros((5, 128), jnp.int32)
     load_table = pltpu.make_async_copy(vtable, table, lsem.at[5])
@@ -202,22 +201,27 @@
     outs[0].start()
     outs[1].start()
 
-    def spread(src_of, dst, send, recv):
+    def spread(src_of, dst, send, recv, start=1, stop=64):
         def to_device(step, _):
-            to = lax.rem(mp + step, 64)
+            to = lax.rem(mp + 37 * step, 64)
             remote(src_of(to), dst, send, recv, k, to).start()
             return 0
 
-        lax.fori_loop(1, 64, to_device, 0)
-        pltpu.make_async_copy(src_of(mp), dst, recv).start()
-
-    spread(
-        lambda to: hpk.at[:, to, pl.ds(0, PIECE), :],
-        hrecv.at[pl.ds(2 * mp, 2), pl.ds(0, PIECE), :],
-        h1sem.at[0],
-        h1sem.at[1],
-    )
-
+        lax.fori_loop(start, stop, to_device, 0)
+        if start == 1:
+            pltpu.make_async_copy(src_of(mp), dst, recv).start()
+
+    def first_hop(start, stop):
+        spread(
+            lambda to: hpk.at[:, to, pl.ds(0, PIECE), :],
+            hrecv.at[pl.ds(2 * mp, 2), pl.ds(0, PIECE), :],
+            h1sem.at[0],
+            h1sem.at[1],
+            start,
+            stop,
+        )
+
+    first_hop(1, 12)
     wait_bytes(act_full.at[:, x, y], zsem.at[1])
     for d in (1, 2, 3):
         to_x = lax.rem(mp + 16 * d, 64)
@@ -226,6 +230,7 @@
         remote(view, view, asem.at[0], asem.at[1], k, to_x).start()
         view = act_full.at[:, x, y, 1]
         remote(view, view, asem.at[2], asem.at[3], k, to_y).start()
+    first_hop(12, 24)
     outs[0].wait_recv()
     ins[0].start()
     swap(inward[0])
@@ -238,12 +243,14 @@
         remote(view, view, asem.at[4], asem.at[5], k, to_y).start()
         view = act_full.at[:, x, :, 1]
         remote(view, view, asem.at[6], asem.at[7], k, to_x).start()
+    first_hop(24, 40)
     outs[1].wait_recv()
     ins[1].start()
     swap(inward[1])
     ins[0].wait_recv()
     outs[2].start()
     swap(cot_rows(e_out, first))
+    first_hop(40, 64)
     load_act.wait()
     down = ((0,), (0,))
     for half in (0, 1):
@@ -265,7 +272,7 @@
         return 0
 
     lax.fori_loop(0, 64, choose, 0)
-    mine = hfin.at[chip, s, pl.ds(0, PIECE), :]
+    mine = hfin.at[mp, pl.ds(0, PIECE), :]
 
     def chosen(g):
         return hsend.at[g, pl.ds(0, PIECE), :]
@@ -320,30 +327,18 @@
     fresh(gtmp, par)
 
     def write_f(n, value):
-        fpk[pl.ds(4 * n, 4), :, pl.ds(0, 16), :] = value.reshape(4, 2, 16, Q)
+        fpk[pl.ds(8 * n, 8), pl.ds(0, 16), :] = value.reshape(8, 16, Q)
 
     def write_f_extra(pair, value):
-        for p in range(32):
-            fpk[p, pair, pl.ds(16, 1), :] = value
+        for p in range(pair, 64, 2):
+            fpk[p, pl.ds(16, 1), :] = value
 
     pack(lambda bi, bj: fbuf[pl.ds(bi * Q, Q), pl.ds(bj * Q, Q)], write_f, write_f_extra)
-    flat = 2 * c + s
-
-    def spread_plane(src_of, dst, send, recv):
-        def to_device(step, _):
-            to = lax.rem(flat + step, 32)
-            to_mp = 4 * lax.div(to, 2) + 2 * zl + lax.rem(to, 2)
-            remote(src_of(to), dst, send, recv, k, to_mp).start()
-            return 0
-
-        lax.fori_loop(1, 32, to_device, 0)
-        pltpu.make_async_copy(src_of(flat), dst, recv).start()
-
-    spread_plane(
-        lambda to: fpk.at[to, :, pl.ds(0, PIECE), :],
-        frecv.at[32 * zl + flat, :, pl.ds(0, PIECE), :],
+    spread(
+        lambda to: fpk.at[to, pl.ds(0, PIECE), :],
+        frecv.at[mp, pl.ds(0, PIECE), :],
         f1sem.at[0],
-        f1sem.at[1 + x],
+        f1sem.at[1],
     )
 
     @pl.when(jnp.logical_not(main))
@@ -351,13 +346,7 @@
         send_g.wait_recv()
         fresh(gp, s)
 
-    for d in (0, 1, 3, 2):
-        from_x = lax.rem(x + d, 4)
-        view = frecv.at[pl.ds(32 * zl + 8 * from_x, 8), :, pl.ds(0, PIECE), :]
-        wait_bytes(view, f1sem.at[1 + from_x])
-        remote(view, view, fwsem.at[0], fwsem.at[1], k, mp2).start()
-
-    wait_bytes(hfin.at[:, :, pl.ds(0, PIECE), :], h2sem.at[1])
+    wait_bytes(hfin.at[:, pl.ds(0, PIECE), :], h2sem.at[1])
 
     def merge(bi, bj, value):
         at = (pl.ds(bi * Q, Q), pl.ds(bj * Q, Q))
@@ -397,6 +386,21 @@
     product(MX, MX, lambda rows, start, value: store(MS, rows, value))
     product(MS, MS, lambda rows, start, value: store(MF, rows, value))
 
+    wait_bytes(frecv.at[:, pl.ds(0, PIECE), :], f1sem.at[1])
+
+    def choose_fresh(o, _):
+        for r in (0, 1):
+            fsend[o, r, pl.ds(0, PIECE), :] = frecv[table[1, 2 * o + r], pl.ds(0, PIECE), :]
+        return 0
+
+    lax.fori_loop(0, 64, choose_fresh, 0)
+    spread(
+        lambda to: fsend.at[to, :, pl.ds(0, PIECE), :],
+        ffin.at[:, mp, pl.ds(0, PIECE), :],
+        f2sem.at[0],
+        f2sem.at[1],
+    )
+
     def next_step(rows, start, value):
         store(MR, rows, value)
         store(MQ, rows, factor(rows, start, value))
@@ -420,23 +424,6 @@
 
     product(MM, MQ, last)
     store(MG, pl.ds(0, B), gp[...])
-
-    wait_bytes(frecv.at[pl.ds(32 - 32 * zl, 32), :, pl.ds(0, PIECE), :], fwsem.at[1])
-
-    def choose_fresh(o, _):
-        owner = 4 * lax.div(o, 2) + 2 * zl + lax.rem(o, 2)
-        for r in (0, 1):
-            g = table[1, 2 * owner + r]
-            fsend[o, r, :, pl.ds(0, PIECE), :] = frecv[g, :, pl.ds(0, PIECE), :]
-        return 0
-
-    lax.fori_loop(0, 32, choose_fresh, 0)
-    spread_plane(
-        lambda to: fsend.at[to, :, :, pl.ds(0, PIECE), :],
-        ffin.at[:, flat, :, pl.ds(0, PIECE), :],
-        f2sem.at[0],
-        f2sem.at[1],
-    )
     for copy in sends_x:
         copy.wait_recv()
 
@@ -458,7 +445,7 @@
 
     pl.when(jnp.logical_not(main))(copies[1].start)
 
-    wait_bytes(ffin.at[:, :, :, pl.ds(0, PIECE), :], f2sem.at[1])
+    wait_bytes(ffin.at[:, :, pl.ds(0, PIECE), :], f2sem.at[1])
     for r in (0, 1):
         used = table[2, 2 * mp + r] > 0
 
@@ -488,9 +475,8 @@
         copy.wait_send()
     wait_bytes(cot_full.at[:, pl.ds(0, 128), :], csem.at[0])
     wait_bytes(hpk.at[:, pl.ds(0, 63), pl.ds(0, PIECE), :], h1sem.at[0])
-    wait_bytes(fpk.at[pl.ds(0, 31), :, pl.ds(0, PIECE), :], f1sem.at[0])
-    wait_bytes(frecv.at[pl.ds(0, 32), :, pl.ds(0, PIECE), :], fwsem.at[0])
-    wait_bytes(fsend.at[pl.ds(0, 31), :, :, pl.ds(0, PIECE), :], f2sem.at[0])
+    wait_bytes(fpk.at[pl.ds(0, 63), pl.ds(0, PIECE), :], f1sem.at[0])
+    wait_bytes(fsend.at[pl.ds(0, 63), :, pl.ds(0, PIECE), :], f2sem.at[0])
     wait_bytes(hsend.at[pl.ds(0, 63), pl.ds(0, PIECE), :], h2sem.at[0])
 
     @pl.when(jnp.logical_not(main))
@@ -507,6 +493,7 @@
 
 
 def body(activations, cotangent, owners, history):
+    hbm = pl.BlockSpec(memory_space=pltpu.HBM)
     anywhere = pl.BlockSpec(memory_space=pl.ANY)
     dma = pltpu.SemaphoreType.DMA
     prec, newh = pl.pallas_call(
@@ -515,7 +502,7 @@
             jax.ShapeDtypeStruct((2, 128, B), f32),
             jax.ShapeDtypeStruct((2, B, B), f32),
         ],
-        in_specs=[anywhere, anywhere, pl.BlockSpec(memory_space=pltpu.VMEM), anywhere],
+        in_specs=[hbm, hbm, pl.BlockSpec(memory_space=pltpu.VMEM), hbm],
         out_specs=[anywhere, anywhere],
         scratch_shapes=[
             pltpu.VMEM((256, B), bf16),
@@ -529,11 +516,11 @@
             pltpu.VMEM((2, 64, 24, Q), f32),
             pltpu.VMEM((128, 24, Q), f32),
             pltpu.VMEM((64, 24, Q), f32),
-            pltpu.VMEM((32, 2, 24, Q), f32),
-            pltpu.VMEM((32, 2, 24, Q), f32),
+            pltpu.VMEM((64, 24, Q), f32),
+            pltpu.VMEM((64, 24, Q), f32),
+            pltpu.VMEM((64, 24, Q), f32),
             pltpu.VMEM((64, 2, 24, Q), f32),
-            pltpu.VMEM((32, 2, 2, 24, Q), f32),
-            pltpu.VMEM((2, 32, 2, 24, Q), f32),
+            pltpu.VMEM((2, 64, 24, Q), f32),
             pltpu.VMEM((B, B), f32),
             pltpu.VMEM((B, B), f32),
             pltpu.VMEM((B, B), f32),
@@ -551,7 +538,6 @@
             dma((2,)),
             dma((2,)),
             dma((2,)),
-            dma((5,)),
             dma((2,)),
             dma((2,)),
             dma((2,)),
@@ -560,7 +546,7 @@
             dma((2,)),
         ],
         compiler_params=pltpu.CompilerParams(
-            collective_id=0, has_side_effects=True, vmem_limit_bytes=62 * 1024 * 1024
+            collective_id=0, has_side_effects=True, vmem_limit_bytes=50 * 1024 * 1024
         ),
     )(activations, cotangent, owners.reshape(1, -1), history[0, 0])
     return prec, newh[None, None]

time: 95.4 us -> 90.9 us (0.953)
  the two profiles are of different devices: /device:TPU:25 before, /device:TPU:4 now
where the time goes in v4:
time: 90.9 us; the launch traced here: 89.8 us
  Pallas kernels  86.4 us (95%)
  local copies, waits for them, and re-layouts  2.76 us (3%)
    pallas_call x1, Pallas kernels, body(): pl.pallas_call(kernel, out_shape=[jax.ShapeDtypeStruct((2, 128, B), f32),...  86.4 us
    unnamed x4, local copies, waits for them, and re-layouts  2.76 us

profile of v4, /device:TPU:4, one launch (start us, length us, event | category | flops | bytes accessed | tf_op | source)
XLA Modules:
  0.0 89.8 jit_solution(13418439940899969392)
XLA Ops:
  0.6 0.0 copy-start
  0.6 0.6 copy-done
  1.3 86.4 %shard_map.59 = (f32[2,128,512]{2,1,0:T(8,128)S(1)}, f32[2,512,512]{2,1,0:T(8,128)S(1)}) custom-call(bf16[256,4096]{1,0:T(8,128)(2,1)} %act.1, bf16[256,8192]{1,0:T(8,128)(2,1)} %cot.1, s32[1,64]{1,0:T(1,128)S(1)} %bitcast.4, f32[2,512,512]{2,1,0:T(8,128)} %bitcast.5), custom_call_target="tpu_custom_call" | custom-call | tf_op jit(solution)/shard_map/pallas_call | solution.py:499
  87.7 0.8 copy.8
  88.5 1.3 %copy.9 = f32[1,1,2,512,512]{4,3,2,1,0:T(8,128)} copy(f32[1,1,2,512,512]{4,3,2,1,0:T(8,128)S(1)} %bitcast.3) | data formatting | bytes 4194304
Async XLA Ops:
  0.6 0.7 copy-start

commit v5 on v4

--- a/solution.py
+++ b/solution.py
@@ -201,27 +201,22 @@
     outs[0].start()
     outs[1].start()
 
-    def spread(src_of, dst, send, recv, start=1, stop=64):
+    def spread(src_of, dst, send, recv):
         def to_device(step, _):
             to = lax.rem(mp + 37 * step, 64)
             remote(src_of(to), dst, send, recv, k, to).start()
             return 0
 
-        lax.fori_loop(start, stop, to_device, 0)
-        if start == 1:
-            pltpu.make_async_copy(src_of(mp), dst, recv).start()
-
-    def first_hop(start, stop):
-        spread(
-            lambda to: hpk.at[:, to, pl.ds(0, PIECE), :],
-            hrecv.at[pl.ds(2 * mp, 2), pl.ds(0, PIECE), :],
-            h1sem.at[0],
-            h1sem.at[1],
-            start,
-            stop,
-        )
-
-    first_hop(1, 12)
+        lax.fori_loop(1, 64, to_device, 0)
+        pltpu.make_async_copy(src_of(mp), dst, recv).start()
+
+    spread(
+        lambda to: hpk.at[:, to, pl.ds(0, PIECE), :],
+        hrecv.at[pl.ds(2 * mp, 2), pl.ds(0, PIECE), :],
+        h1sem.at[0],
+        h1sem.at[1],
+    )
+
     wait_bytes(act_full.at[:, x, y], zsem.at[1])
     for d in (1, 2, 3):
         to_x = lax.rem(mp + 16 * d, 64)
@@ -230,7 +225,6 @@
         remote(view, view, asem.at[0], asem.at[1], k, to_x).start()
         view = act_full.at[:, x, y, 1]
         remote(view, view, asem.at[2], asem.at[3], k, to_y).start()
-    first_hop(12, 24)
     outs[0].wait_recv()
     ins[0].start()
     swap(inward[0])
@@ -243,14 +237,12 @@
         remote(view, view, asem.at[4], asem.at[5], k, to_y).start()
         view = act_full.at[:, x, :, 1]
         remote(view, view, asem.at[6], asem.at[7], k, to_x).start()
-    first_hop(24, 40)
     outs[1].wait_recv()
     ins[1].start()
     swap(inward[1])
     ins[0].wait_recv()
     outs[2].start()
     swap(cot_rows(e_out, first))
-    first_hop(40, 64)
     load_act.wait()
     down = ((0,), (0,))
     for half in (0, 1):

time: 90.9 us -> 87.9 us (0.967)
  Pallas kernels: 86.4 us -> 83.6 us
    pallas_call x1, Pallas kernels: 86.4 us -> 83.6 us  [body(): pl.pallas_call(kernel, out_shape=[jax.ShapeDtypeStruct((2, 128, B), f32),...]
where the time goes in v5:
time: 87.9 us; the launch traced here: 87 us
  Pallas kernels  83.6 us (95%)
  local copies, waits for them, and re-layouts  2.76 us (3%)
    pallas_call x1, Pallas kernels, body(): pl.pallas_call(kernel, out_shape=[jax.ShapeDtypeStruct((2, 128, B), f32),...  83.6 us
    unnamed x4, local copies, waits for them, and re-layouts  2.76 us

profile of v5, /device:TPU:4, one launch (start us, length us, event | category | flops | bytes accessed | tf_op | source)
XLA Modules:
  0.0 87.0 jit_solution(193784103161842613)
XLA Ops:
  0.6 0.0 copy-start
  0.6 0.6 copy-done
  1.3 83.6 %shard_map.59 = (f32[2,128,512]{2,1,0:T(8,128)S(1)}, f32[2,512,512]{2,1,0:T(8,128)S(1)}) custom-call(bf16[256,4096]{1,0:T(8,128)(2,1)} %act.1, bf16[256,8192]{1,0:T(8,128)(2,1)} %cot.1, s32[1,64]{1,0:T(1,128)S(1)} %bitcast.4, f32[2,512,512]{2,1,0:T(8,128)} %bitcast.5), custom_call_target="tpu_custom_call" | custom-call | tf_op jit(solution)/shard_map/pallas_call | solution.py:491
  84.9 0.8 copy.8
  85.7 1.3 %copy.9 = f32[1,1,2,512,512]{4,3,2,1,0:T(8,128)} copy(f32[1,1,2,512,512]{4,3,2,1,0:T(8,128)S(1)} %bitcast.3) | data formatting | bytes 4194304
Async XLA Ops:
  0.6 0.7 copy-start

commit v6 on v5

--- a/solution.py
+++ b/solution.py
@@ -8,7 +8,7 @@
 B = 512
 Q = 128
 ABOVE = [(0, 1), (0, 2), (0, 3), (1, 2), (1, 3), (2, 3)]
-PIECE = 17
+PIECE, EXTRA = 16, 17
 f32 = jnp.float32
 bf16 = jnp.bfloat16
 
@@ -69,7 +69,7 @@
     act, cot, owner_row, hist, prec, newh,
     act_own, act_part, cot_own, zact, zcot, act_full, cot_full,
     hv, hpk, hrecv, hsend, hfin, fpk, frecv, fsend, ffin,
-    gtmp, gp, fbuf, xs, mats, pbuf, pfin, vtable, table,
+    gtmp, gp, fbuf, xs, mats, pbuf, pfin, vtable, table, ruler,
     lsem, zsem, asem, osem, isem, csem, h1sem, h2sem, f1sem, f2sem, gsem, xsem, psend, precv,
 ):
     k = lax.axis_index("dp")
@@ -140,6 +140,66 @@
         copy.wait()
     zact[...] = act_part[...].astype(f32).reshape(2, 2, 8, B)
     zcot[...] = cot_own[pl.ds(pl.multiple_of(s * 128, 128), 128), :].astype(f32).reshape(2, 64, B)
+    pl.semaphore_wait(barrier, 132)
+
+    for e in (1, 2, 3):
+        to = lax.rem(k + e, 4)
+        remote(
+            zact.at[lax.div(to, 2)], act_full.at[3 - e, x, y], zsem.at[0], zsem.at[1], to, mp
+        ).start()
+
+    def cot_rows(e, half):
+        return cot_full.at[e, pl.ds(pl.multiple_of(s * 128 + half * 64, 64), 64), :]
+
+    out_dp = lax.rem(k + 3 + 2 * zl, 4)
+    e_out, e_in = 2 * zl, 2 - 2 * zl
+    first, second = 1 - zl, zl
+    outs = [
+        remote(zcot.at[first], cot_rows(e_out, first), osem.at[0], osem.at[3], out_dp, mp2),
+        remote(zcot.at[second], cot_rows(e_out, second), osem.at[1], osem.at[4], out_dp, mp2),
+        remote(cot_rows(e_out, first), cot_rows(1, first), osem.at[2], osem.at[5], out_dp, mp2),
+    ]
+    inward = [cot_rows(e_in, second), cot_rows(e_in, first), cot_rows(1, second)]
+    ins = [
+        remote(view, view, isem.at[n], isem.at[3 + n], k, mp2) for n, view in enumerate(inward)
+    ]
+
+    def swap(view):
+        remote(view, view, csem.at[0], csem.at[1], k, mp1).start()
+
+    outs[0].start()
+    outs[1].start()
+
+    load_hist.wait()
+    for r in (0, 1):
+
+        def write(n, value, r=r):
+            hpk[r, pl.ds(8 * n, 8), pl.ds(0, 16), :] = value.reshape(8, 16, Q)
+
+        def write_extra(pair, value, r=r):
+            hpk[r, pair, pl.ds(16, 1), :] = value
+
+        pack(lambda bi, bj, r=r: hv[r, pl.ds(bi * Q, Q), pl.ds(bj * Q, Q)], write, write_extra)
+    def sized(device, fn):
+        pl.when(device < 2)(lambda: fn(EXTRA))
+        pl.when(device >= 2)(lambda: fn(PIECE))
+
+    def spread(src_of, dst_of, send, recv):
+        def to_device(step, _):
+            to = lax.rem(mp + 37 * step, 64)
+            sized(to, lambda n: remote(src_of(to, n), dst_of(n), send, recv, k, to).start())
+            return 0
+
+        lax.fori_loop(1, 64, to_device, 0)
+        sized(mp, lambda n: pltpu.make_async_copy(src_of(mp, n), dst_of(n), recv).start())
+
+    spread(
+        lambda to, n: hpk.at[:, to, pl.ds(0, n), :],
+        lambda n: hrecv.at[pl.ds(2 * mp, 2), pl.ds(0, n), :],
+        h1sem.at[0],
+        h1sem.at[1],
+    )
+
     own_row = jnp.broadcast_to(owner_row[...], (128, 64))
     own_col = jnp.transpose(own_row)
     own_row = own_row[0:64, :]
@@ -160,63 +220,6 @@
     vtable[3:8, :] = jnp.zeros((5, 128), jnp.int32)
     load_table = pltpu.make_async_copy(vtable, table, lsem.at[5])
     load_table.start()
-    load_hist.wait()
-    for r in (0, 1):
-
-        def write(n, value, r=r):
-            hpk[r, pl.ds(8 * n, 8), pl.ds(0, 16), :] = value.reshape(8, 16, Q)
-
-        def write_extra(pair, value, r=r):
-            for p in range(pair, 64, 2):
-                hpk[r, p, pl.ds(16, 1), :] = value
-
-        pack(lambda bi, bj, r=r: hv[r, pl.ds(bi * Q, Q), pl.ds(bj * Q, Q)], write, write_extra)
-    pl.semaphore_wait(barrier, 132)
-
-    for e in (1, 2, 3):
-        to = lax.rem(k + e, 4)
-        remote(
-            zact.at[lax.div(to, 2)], act_full.at[3 - e, x, y], zsem.at[0], zsem.at[1], to, mp
-        ).start()
-
-    def cot_rows(e, half):
-        return cot_full.at[e, pl.ds(pl.multiple_of(s * 128 + half * 64, 64), 64), :]
-
-    out_dp = lax.rem(k + 3 + 2 * zl, 4)
-    e_out, e_in = 2 * zl, 2 - 2 * zl
-    first, second = 1 - zl, zl
-    outs = [
-        remote(zcot.at[first], cot_rows(e_out, first), osem.at[0], osem.at[3], out_dp, mp2),
-        remote(zcot.at[second], cot_rows(e_out, second), osem.at[1], osem.at[4], out_dp, mp2),
-        remote(cot_rows(e_out, first), cot_rows(1, first), osem.at[2], osem.at[5], out_dp, mp2),
-    ]
-    inward = [cot_rows(e_in, second), cot_rows(e_in, first), cot_rows(1, second)]
-    ins = [
-        remote(view, view, isem.at[n], isem.at[3 + n], k, mp2) for n, view in enumerate(inward)
-    ]
-
-    def swap(view):
-        remote(view, view, csem.at[0], csem.at[1], k, mp1).start()
-
-    outs[0].start()
-    outs[1].start()
-
-    def spread(src_of, dst, send, recv):
-        def to_device(step, _):
-            to = lax.rem(mp + 37 * step, 64)
-            remote(src_of(to), dst, send, recv, k, to).start()
-            return 0
-
-        lax.fori_loop(1, 64, to_device, 0)
-        pltpu.make_async_copy(src_of(mp), dst, recv).start()
-
-    spread(
-        lambda to: hpk.at[:, to, pl.ds(0, PIECE), :],
-        hrecv.at[pl.ds(2 * mp, 2), pl.ds(0, PIECE), :],
-        h1sem.at[0],
-        h1sem.at[1],
-    )
-
     wait_bytes(act_full.at[:, x, y], zsem.at[1])
     for d in (1, 2, 3):
         to_x = lax.rem(mp + 16 * d, 64)
@@ -257,35 +260,38 @@
     swap(cot_rows(1, first))
 
     load_table.wait()
-    wait_bytes(hrecv.at[:, pl.ds(0, PIECE), :], h1sem.at[1])
-
-    def choose(g, _):
-        hsend[g, pl.ds(0, PIECE), :] = hrecv[table[0, g], pl.ds(0, PIECE), :]
-        return 0
-
-    lax.fori_loop(0, 64, choose, 0)
-    mine = hfin.at[mp, pl.ds(0, PIECE), :]
-
-    def chosen(g):
-        return hsend.at[g, pl.ds(0, PIECE), :]
-
-    def to_chip(step, _):
-        to = 2 * lax.rem(chip + step, 32)
-        remote(chosen(to + par), mine, h2sem.at[0], h2sem.at[1], k, to + par).start()
-        remote(chosen(to + 1 - par), mine, h2sem.at[0], h2sem.at[1], k1, to + par).start()
-        return 0
-
-    lax.fori_loop(1, 32, to_chip, 0)
-    here = 2 * chip
-    remote(chosen(here + 1 - par), mine, h2sem.at[0], h2sem.at[1], k1, here + par).start()
-
-    @pl.when(main)
-    def _():
-        pltpu.make_async_copy(chosen(here + par), mine, h2sem.at[1]).start()
-
-    @pl.when(jnp.logical_not(main))
-    def _():
-        remote(chosen(here + par), mine, h2sem.at[0], h2sem.at[1], k, mp1).start()
+    def second_hop(n):
+        wait_bytes(hrecv.at[:, pl.ds(0, n), :], h1sem.at[1])
+        mine = hfin.at[mp, pl.ds(0, n), :]
+
+        def choose(g):
+            hsend[g, pl.ds(0, n), :] = hrecv[table[0, g], pl.ds(0, n), :]
+            return hsend.at[g, pl.ds(0, n), :]
+
+        def to_chip_beyond(step, _):
+            to = 2 * lax.rem(chip + step, 32)
+            src = choose(to + 1 - par)
+            remote(src, mine, h2sem.at[0], h2sem.at[1], k1, to + par).start()
+            return 0
+
+        def to_chip(step, _):
+            to = 2 * lax.rem(chip + step, 32)
+            remote(choose(to + par), mine, h2sem.at[0], h2sem.at[1], k, to + par).start()
+            return 0
+
+        lax.fori_loop(0, 32, to_chip_beyond, 0)
+        lax.fori_loop(1, 32, to_chip, 0)
+        src = choose(2 * chip + par)
+
+        @pl.when(main)
+        def _():
+            pltpu.make_async_copy(src, mine, h2sem.at[1]).start()
+
+        @pl.when(jnp.logical_not(main))
+        def _():
+            remote(src, mine, h2sem.at[0], h2sem.at[1], k, mp1).start()
+
+    sized(mp, second_hop)
 
     wait_bytes(act_full.at[:, pl.ds(0, 3), :, 0], asem.at[5])
     wait_bytes(act_full.at[:, pl.ds(0, 3), :, 0], asem.at[7])
@@ -322,13 +328,12 @@
         fpk[pl.ds(8 * n, 8), pl.ds(0, 16), :] = value.reshape(8, 16, Q)
 
     def write_f_extra(pair, value):
-        for p in range(pair, 64, 2):
-            fpk[p, pl.ds(16, 1), :] = value
+        fpk[pair, pl.ds(16, 1), :] = value
 
     pack(lambda bi, bj: fbuf[pl.ds(bi * Q, Q), pl.ds(bj * Q, Q)], write_f, write_f_extra)
     spread(
-        lambda to: fpk.at[to, pl.ds(0, PIECE), :],
-        frecv.at[mp, pl.ds(0, PIECE), :],
+        lambda to, n: fpk.at[to, pl.ds(0, n), :],
+        lambda n: frecv.at[mp, pl.ds(0, n), :],
         f1sem.at[0],
         f1sem.at[1],
     )
@@ -338,7 +343,7 @@
         send_g.wait_recv()
         fresh(gp, s)
 
-    wait_bytes(hfin.at[:, pl.ds(0, PIECE), :], h2sem.at[1])
+    wait_bytes(ruler.at[pl.ds(0, 1026), :], h2sem.at[1])
 
     def merge(bi, bj, value):
         at = (pl.ds(bi * Q, Q), pl.ds(bj * Q, Q))
@@ -378,20 +383,24 @@
     product(MX, MX, lambda rows, start, value: store(MS, rows, value))
     product(MS, MS, lambda rows, start, value: store(MF, rows, value))
 
-    wait_bytes(frecv.at[:, pl.ds(0, PIECE), :], f1sem.at[1])
-
-    def choose_fresh(o, _):
-        for r in (0, 1):
-            fsend[o, r, pl.ds(0, PIECE), :] = frecv[table[1, 2 * o + r], pl.ds(0, PIECE), :]
-        return 0
-
-    lax.fori_loop(0, 64, choose_fresh, 0)
-    spread(
-        lambda to: fsend.at[to, :, pl.ds(0, PIECE), :],
-        ffin.at[:, mp, pl.ds(0, PIECE), :],
-        f2sem.at[0],
-        f2sem.at[1],
-    )
+    def owners_hop(n):
+        wait_bytes(frecv.at[:, pl.ds(0, n), :], f1sem.at[1])
+        mine = ffin.at[:, mp, pl.ds(0, n), :]
+
+        def choose(o):
+            for r in (0, 1):
+                fsend[o, r, pl.ds(0, n), :] = frecv[table[1, 2 * o + r], pl.ds(0, n), :]
+            return fsend.at[o, :, pl.ds(0, n), :]
+
+        def to_owner(step, _):
+            o = lax.rem(mp + 37 * step, 64)
+            remote(choose(o), mine, f2sem.at[0], f2sem.at[1], k, o).start()
+            return 0
+
+        lax.fori_loop(1, 64, to_owner, 0)
+        pltpu.make_async_copy(choose(mp), mine, f2sem.at[1]).start()
+
+    sized(mp, owners_hop)
 
     def next_step(rows, start, value):
         store(MR, rows, value)
@@ -437,7 +446,7 @@
 
     pl.when(jnp.logical_not(main))(copies[1].start)
 
-    wait_bytes(ffin.at[:, :, pl.ds(0, PIECE), :], f2sem.at[1])
+    wait_bytes(ruler.at[pl.ds(0, 2052), :], f2sem.at[1])
     for r in (0, 1):
         used = table[2, 2 * mp + r] > 0
 
@@ -466,15 +475,18 @@
     for copy in outs + ins:
         copy.wait_send()
     wait_bytes(cot_full.at[:, pl.ds(0, 128), :], csem.at[0])
-    wait_bytes(hpk.at[:, pl.ds(0, 63), pl.ds(0, PIECE), :], h1sem.at[0])
-    wait_bytes(fpk.at[pl.ds(0, 63), pl.ds(0, PIECE), :], f1sem.at[0])
-    wait_bytes(fsend.at[pl.ds(0, 63), :, pl.ds(0, PIECE), :], f2sem.at[0])
-    wait_bytes(hsend.at[pl.ds(0, 63), pl.ds(0, PIECE), :], h2sem.at[0])
-
-    @pl.when(jnp.logical_not(main))
-    def _():
-        wait_bytes(hsend.at[0, pl.ds(0, PIECE), :], h2sem.at[0])
-
+    def sent(n):
+        total = 63 * PIECE + (1 if n == EXTRA else 2)
+        wait_bytes(ruler.at[pl.ds(0, 2 * total), :], h1sem.at[0])
+        wait_bytes(ruler.at[pl.ds(0, total), :], f1sem.at[0])
+        wait_bytes(fsend.at[pl.ds(0, 63), :, pl.ds(0, n), :], f2sem.at[0])
+        wait_bytes(hsend.at[pl.ds(0, 63), pl.ds(0, n), :], h2sem.at[0])
+
+        @pl.when(jnp.logical_not(main))
+        def _():
+            wait_bytes(hsend.at[0, pl.ds(0, n), :], h2sem.at[0])
+
+    sized(mp, sent)
     pl.when(main)(send_g.wait_send)
     for copy in sends_x:
         copy.wait_send()
@@ -522,6 +534,7 @@
             pltpu.VMEM((2, 128, B), f32),
             pltpu.VMEM((8, 128), jnp.int32),
             pltpu.SMEM((8, 128), jnp.int32),
+            pltpu.VMEM((2056, Q), f32),
             dma((6,)),
             dma((2,)),
             dma((8,)),

time: 87.9 us -> 85.4 us (0.972)
  Pallas kernels: 83.6 us -> 80.7 us
    pallas_call x1, Pallas kernels: 83.6 us -> 80.7 us  [body(): pl.pallas_call(kernel, out_shape=[jax.ShapeDtypeStruct((2, 128, B), f32),...]
where the time goes in v6:
time: 85.4 us; the launch traced here: 84.1 us
  Pallas kernels  80.7 us (94%)
  local copies, waits for them, and re-layouts  2.76 us (3%)
    pallas_call x1, Pallas kernels, body(): pl.pallas_call(kernel, out_shape=[jax.ShapeDtypeStruct((2, 128, B), f32),...  80.7 us
    unnamed x4, local copies, waits for them, and re-layouts  2.76 us

profile of v6, /device:TPU:4, one launch (start us, length us, event | category | flops | bytes accessed | tf_op | source)
XLA Modules:
  0.0 84.1 jit_solution(9660647148917524942)
XLA Ops:
  0.6 0.0 copy-start
  0.6 0.6 copy-done
  1.3 80.7 %shard_map.59 = (f32[2,128,512]{2,1,0:T(8,128)S(1)}, f32[2,512,512]{2,1,0:T(8,128)S(1)}) custom-call(bf16[256,4096]{1,0:T(8,128)(2,1)} %act.1, bf16[256,8192]{1,0:T(8,128)(2,1)} %cot.1, s32[1,64]{1,0:T(1,128)S(1)} %bitcast.4, f32[2,512,512]{2,1,0:T(8,128)} %bitcast.5), custom_call_target="tpu_custom_call" | custom-call | tf_op jit(solution)/shard_map/pallas_call | solution.py:503
  82.0 0.8 copy.8
  82.8 1.3 %copy.9 = f32[1,1,2,512,512]{4,3,2,1,0:T(8,128)} copy(f32[1,1,2,512,512]{4,3,2,1,0:T(8,128)S(1)} %bitcast.3) | data formatting | bytes 4194304
Async XLA Ops:
  0.6 0.7 copy-start

commit v7 on v6

--- a/solution.py
+++ b/solution.py
@@ -366,13 +366,13 @@
         return jnp.where(row == col, 1.25, 0.0) - 0.25 * value
 
     def product(a, b, after):
-        for start in (0, 256):
-            rows = pl.ds(start, 256)
-            after(
-                rows,
-                start,
-                dot3(mats[a, rows, :], mats[a + 1, rows, :], mats[b], mats[b + 1]),
-            )
+        top, low = pl.ds(0, 256), pl.ds(256, 256)
+        first = dot3(mats[a, top, :], mats[a + 1, top, :], mats[b], mats[b + 1])
+        after(top, 0, first)
+        last = dot3(
+            mats[a, low, :], mats[a + 1, low, :], mats[b, :, low], mats[b + 1, :, low]
+        )
+        after(low, 256, jnp.concatenate([first[:, 256:].T, last], axis=1))
 
     MG, MQ, MS, MF, MM, MX, MR = 0, 2, 4, 6, 8, 10, 12
     for start in (0, 256):

time: 85.4 us -> 85.4 us (level)
  no operation moved by 1% of the time
where the time goes in v7:
time: 85.4 us; the launch traced here: 84.1 us
  Pallas kernels  80.7 us (94%)
  local copies, waits for them, and re-layouts  2.76 us (3%)
    pallas_call x1, Pallas kernels, body(): pl.pallas_call(kernel, out_shape=[jax.ShapeDtypeStruct((2, 128, B), f32),...  80.7 us
    unnamed x4, local copies, waits for them, and re-layouts  2.76 us

profile of v7, /device:TPU:4, one launch (start us, length us, event | category | flops | bytes accessed | tf_op | source)
XLA Modules:
  0.0 84.1 jit_solution(8132379052894922386)
XLA Ops:
  0.6 0.0 copy-start
  0.6 0.6 copy-done
  1.3 80.7 %shard_map.59 = (f32[2,128,512]{2,1,0:T(8,128)S(1)}, f32[2,512,512]{2,1,0:T(8,128)S(1)}) custom-call(bf16[256,4096]{1,0:T(8,128)(2,1)} %act.1, bf16[256,8192]{1,0:T(8,128)(2,1)} %cot.1, s32[1,64]{1,0:T(1,128)S(1)} %bitcast.4, f32[2,512,512]{2,1,0:T(8,128)} %bitcast.5), custom_call_target="tpu_custom_call" | custom-call | tf_op jit(solution)/shard_map/pallas_call | solution.py:503
  82.0 0.8 copy.8
  82.8 1.3 %copy.9 = f32[1,1,2,512,512]{4,3,2,1,0:T(8,128)} copy(f32[1,1,2,512,512]{4,3,2,1,0:T(8,128)S(1)} %bitcast.3) | data formatting | bytes 4194304
Async XLA Ops:
  0.6 0.7 copy-start
